TPU v7x, 256 devices: a whole 4x4x8 slice. The times are simulated.
256 devices in a mesh: dp: 16 (over z_hi, x, core), cent: 16 (over z_lo, y).
Axes of the slice: x: 4, y: 4, z: 8 (z_hi: 2, z_lo: 4; z = z_hi * 4 + z_lo), core: 2. Of those that a mesh axis runs over, the one named last changes fastest.
Arguments:
- points: bfloat16 [16384, 1024], P('dp'), may hold values from -6 to 6
- cent_one: bfloat16 [32768, 1024], P('cent'), may hold values from -6 to 6
- cent_two: bfloat16 [2048, 1024], replicated, may hold values from -6 to 6
Outputs:
- new_one: bfloat16 [32768, 1024], P('cent', 'dp')
- new_two: bfloat16 [2048, 1024], P(('dp', 'cent'))
All inputs are finite; a program needn't handle non-finite values.
Results may differ from a plain program's by a relative error of at most 0.003.
Values may be sent and summed in bfloat16 or wider, within the bound.
No kernel may reach another device: no remote copies, remote signals or barrier semaphores. Data moves between devices by JAX's collectives and lax.ppermute only.
A program may use at most 64 MiB of HBM per device.

v0:
```python
import functools

import jax
import jax.numpy as jnp
from jax import lax
from jax.experimental import pallas as pl
from jax.experimental.pallas import tpu as pltpu
from jax.sharding import Mesh, PartitionSpec as P

prior_one = 0.5
prior_two = 2.0
sharp_two = 0.25

CENT = ("zl", "y")
ALL = ("zh", "x", "core", "zl", "y")
HOPS = (2, 1, 3, 0)
EXTRA = 16
VMEM = 32 * 2**20
HBM = pl.BlockSpec(memory_space=pltpu.HBM)
f32 = jnp.float32
bf16 = jnp.bfloat16


def swap(v, axis):
    return lax.all_to_all(v, axis, 0, 0, tiled=True)


def shift(v, axis, n, k):
    return lax.ppermute(v, axis, [(i, (i + k) % n) for i in range(n)])


def far(v):
    return pltpu.with_memory_space_constraint(v, pltpu.HBM)


def dot(a, b, dims):
    return lax.dot_general(a, b, (dims, ((), ())), preferred_element_type=f32)


def with_mass(v, block):
    mass = v[block : block + 1] + v[block + 1 : block + 2]
    rounded = lax.reduce_precision(mass, 8, 7)
    line = lax.broadcasted_iota(jnp.int32, v.shape, 0)
    v = jnp.where(line == block, rounded, jnp.where(line == block + 1, mass - rounded, v))
    return v.astype(bf16)


def with_mass_columns(v, half):
    mass = v[:, half : half + 1] + v[:, half + 1 : half + 2]
    rounded = lax.reduce_precision(mass, 8, 7)
    lane = lax.broadcasted_iota(jnp.int32, v.shape, 1)
    v = jnp.where(lane == half, rounded, jnp.where(lane > half, mass - rounded, v))
    return v.astype(bf16)


def log_total(scores):
    high = jnp.max(scores, axis=0)
    return high + jnp.log(jnp.sum(jnp.exp(scores - high), axis=0))


def sums_kernel(index, e_mine, e_other, f_mine, f_other, p_mine, p_other, *refs):
    outs, (weights, lanes, e_held, p_held, e_sem, p_sem) = refs[:4], refs[4:]
    block = outs[0].shape[0] - EXTRA
    count, width = p_mine.shape
    def e_copy(i, j, e):
        at = pl.ds(pl.multiple_of(index[i] * block, block), block)
        return pltpu.make_async_copy(e.at[at, :], e_held.at[j, i], e_sem.at[j, i])

    p_copies = [
        pltpu.make_async_copy(p, p_held.at[j], p_sem.at[j]) for j, p in enumerate((p_mine, p_other))
    ]
    for i in range(4):
        for j, e in enumerate((e_mine, e_other)):
            e_copy(i, j, e).start()
    for copy in p_copies:
        copy.start()

    def fill(i, carry):
        to = pl.ds(pl.multiple_of(i * block, block), block)
        lane = 0.0
        for j, (e, f) in enumerate(((e_mine, f_mine), (e_other, f_other))):
            e_copy(i, j, e).wait()
            w = e_held[j, i].astype(f32) * f[...]
            for n in range(count // 128):
                lane = lane + w[:, n * 128 : (n + 1) * 128]
            weights[to, j * count : (j + 1) * count] = w.astype(bf16)
        lanes[to, :] = lane
        return carry

    lax.fori_loop(0, 4, fill, 0)
    mass = jnp.sum(lanes[...].T, axis=0, keepdims=True)
    line = lax.broadcasted_iota(jnp.int32, (EXTRA, block), 0)
    for copy in p_copies:
        copy.wait()

    def tile(n, carry):
        cols = pl.ds(pl.multiple_of(n * (width // 4), width // 4), width // 4)
        v = dot(weights[:, :count], p_held[0, :, cols], ((1,), (0,)))
        v += dot(weights[:, count:], p_held[1, :, cols], ((1,), (0,)))
        for i, ref in enumerate(outs):
            ref[:block, cols] = v[i * block : (i + 1) * block, :].astype(ref.dtype)
        return carry

    lax.fori_loop(0, 4, tile, 0)
    for i, ref in enumerate(outs):
        m = jnp.broadcast_to(mass[:, i * block : (i + 1) * block], (EXTRA, block))
        r = m.astype(ref.dtype).astype(f32)
        m = jnp.where(line == 0, r, jnp.where(line == 1, m - r, 0.0)).astype(ref.dtype)
        ref[block:, :] = jnp.concatenate([m] * (width // block), axis=1)


def level_one_sums(index, e, factors, points):
    count, width = points[0].shape
    total = e[0].shape[0]
    block = total // 8
    types = [bf16] * 3 + [f32]
    vmem = pl.BlockSpec(memory_space=pltpu.VMEM)
    return pl.pallas_call(
        sums_kernel,
        in_specs=[pl.BlockSpec(memory_space=pltpu.SMEM)] + [HBM] * 2 + [vmem] * 2 + [HBM] * 2,
        out_specs=[vmem] * 4,
        scratch_shapes=[
            pltpu.VMEM((4 * block, 2 * count), bf16),
            pltpu.VMEM((4 * block, 128), f32),
            pltpu.VMEM((2, 4, block, count), bf16),
            pltpu.VMEM((2, count, width), bf16),
            pltpu.SemaphoreType.DMA((2, 4)),
            pltpu.SemaphoreType.DMA((2,)),
        ],
        out_shape=[jax.ShapeDtypeStruct((block + EXTRA, width), t) for t in types],
        compiler_params=pltpu.CompilerParams(vmem_limit_bytes=VMEM),
        cost_estimate=pl.CostEstimate(
            flops=2 * total * count * width,
            bytes_accessed=2 * count * (total + 2 * width) + 2 * total * width,
            transcendentals=0,
        ),
        name="level_one_sums",
    )(index, *map(far, e), *factors, *map(far, points))


def level_two_kernel(
    keep, place, rows_mine, rows_other, mass, table_far, *refs
):
    outs, (rows, turned, second, spread, table, sem) = refs[:8], refs[8:]
    block, width = rows_mine.shape
    count = table.shape[0]
    part = lambda i: pl.ds(pl.multiple_of(i * (count // 4), count // 4), count // 4)
    copy = lambda i: pltpu.make_async_copy(table_far.at[part(i), :], table.at[part(i), :], sem.at[i])
    for i in range(4):
        copy(i).start()
    rows[:block, :width] = rows_mine[...]
    rows[block:, :width] = rows_other[...]
    rows[:, width:] = jnp.ones((2 * block, 128), bf16)
    turned[...] = rows[:, :width].astype(f32).T.astype(bf16)

    def scores(i, high):
        copy(i).wait()
        at = part(i)
        wide = table[at, :].astype(f32)
        sq = jnp.sum(wide * wide, axis=1, keepdims=True) * sharp_two
        v = dot(table[at, :], turned[...], ((1,), (0,))) * (2.0 * sharp_two) - sq
        second[at, :] = v
        return jnp.maximum(high, jnp.max(v, axis=0, keepdims=True))

    high = lax.fori_loop(0, 4, scores, jnp.full((1, 2 * block), -jnp.inf, f32))

    def powers(i, total):
        v = jnp.exp(second[part(i), :] - high)
        second[part(i), :] = v
        return total + jnp.sum(v, axis=0, keepdims=True)

    total = lax.fori_loop(0, 4, powers, jnp.zeros((1, 2 * block), f32))
    weight = mass[...] / total
    half = width // 2
    lane = lax.broadcasted_iota(jnp.int32, (8 * 4 * keep, 128), 1)
    for i in range(4):
        for color in range(2):
            for j in range(4):
                to_x, to_y = (i, j) if color == 0 else (j, i)
                start = place[0] + (place[1 + to_x] * 32 + place[5 + to_y]) * keep
                starts = [start + (zh * 128 + zl * 4) * keep for zh in range(2) for zl in range(4)]
                v = [second[pl.ds(pl.multiple_of(s, keep), keep), :] for s in starts]
                to = slice(j * 8 * keep, (j + 1) * 8 * keep)
                spread[2 * i + color, to, :] = (jnp.concatenate(v) * weight).astype(bf16)
            cols = slice(0, half) if color == 0 else slice(half, width + 128)
            v = dot(spread[2 * i + color], rows[:, cols], ((1,), (0,)))
            out = outs[4 * color + i]
            if color == 0:
                out[...] = v.astype(out.dtype)
                continue
            r = v.astype(out.dtype)
            out[:, :half] = r[:, :half]
            left = (v[:, half:] - r[:, half:].astype(f32)).astype(out.dtype)
            out[:, half:] = jnp.where(lane > 0, left, r[:, half:])


def level_two_sums(place, rows_mine, rows_other, mass, table):
    block, width = rows_mine.shape
    count = table.shape[0]
    vmem = pl.BlockSpec(memory_space=pltpu.VMEM)
    return pl.pallas_call(
        functools.partial(level_two_kernel, count // 256),
        in_specs=[pl.BlockSpec(memory_space=pltpu.SMEM)] + [vmem] * 3 + [HBM],
        out_specs=[vmem] * 8,
        scratch_shapes=[
            pltpu.VMEM((2 * block, width + 128), bf16),
            pltpu.VMEM((width, 2 * block), bf16),
            pltpu.VMEM((count, 2 * block), f32),
            pltpu.VMEM((8, count // 8, 2 * block), bf16),
            pltpu.VMEM((count, width), bf16),
            pltpu.SemaphoreType.DMA((4,)),
        ],
        out_shape=[
            jax.ShapeDtypeStruct((count // 8, cols), t)
            for cols in (width // 2, width // 2 + 128)
            for t in (bf16, bf16, bf16, f32)
        ],
        compiler_params=pltpu.CompilerParams(vmem_limit_bytes=VMEM),
        cost_estimate=pl.CostEstimate(
            flops=8 * block * count * width,
            bytes_accessed=4 * count * width,
            transcendentals=2 * block * count,
        ),
        name="level_two_sums",
    )(place, rows_mine, rows_other, mass, far(table))


def on_device(points, cent_one, cent_two):
    width = points.shape[1]
    core, x, y, zh = [lax.axis_index(name) for name in ("core", "x", "y", "zh")]
    block = cent_one.shape[0] // 16

    scale = 0.5 * width ** (-0.5)

    with jax.named_scope("scores_one"):
        pts = (points, shift(points, "core", 2, 1))
        cents = lax.dynamic_slice_in_dim(cent_one, core * (8 * block), 8 * block, 0)
        sq = jnp.sum(jnp.square(cents.astype(f32)), axis=1)[:, None]

        def level_one_scores(p):
            scores = (2.0 * dot(cents, p, ((1,), (1,))) - sq) * scale
            high = jnp.max(scores, axis=0)
            e = jnp.exp(scores - high)
            return e.astype(bf16), high, high + jnp.log(jnp.sum(e, axis=0))

        first = level_one_scores(points)
        other, first = lax.optimization_barrier((pts[1], first))
        pts = (points, other)
        e, highs, sums = zip(first, level_one_scores(other))
    with jax.named_scope("exchange_softmax"):
        mine = log_total(jnp.stack([sums[0], shift(sums[1], "core", 2, 1)]))
        mine = log_total(swap(jnp.broadcast_to(mine, (16,) + mine.shape), CENT))
        norms = (mine, shift(mine, "core", 2, 1))
        factors = [jnp.exp(h - n)[None] for h, n in zip(highs, norms)]
    with jax.named_scope("reduce_one"):
        sums = []
        for z in (1 - zh, zh):
            index = ((x + jnp.array(HOPS, jnp.int32)) % 4) * 2 + z
            *sent, own = level_one_sums(index, e, factors, pts)
            got = [shift(v, "x", 4, k) for v, k in zip(sent, HOPS)]
            sums.append(own + sum(g.astype(f32) for g in got))
        part = sums[1] + lax.ppermute(with_mass(sums[0], block), "zh", [(0, 1), (1, 0)]).astype(f32)
    with jax.named_scope("finish_one"):
        mass = (part[block] + part[block + 1])[:block]
        place = ((core * 4 + x) * 2 + zh) * block
        old = lax.dynamic_slice_in_dim(cent_one, place, block, 0).astype(f32)
        rows = ((part[:block] + prior_one * old) / (mass[:, None] + prior_one)).astype(bf16)
        rows_other = shift(rows, "core", 2, 1)
        mass_all = jnp.stack([mass, shift(mass, "core", 2, 1)]).reshape(1, 2 * block)
    with jax.named_scope("scores_two"):
        keep = cent_two.shape[0] // 256
        hops = jnp.array(HOPS, jnp.int32)
        place = jnp.concatenate([(core * 16 * keep).reshape(1), (x + hops) % 4, (y + hops) % 4])
        parts = level_two_sums(place, rows, rows_other, mass_all, cent_two)
    with jax.named_scope("reduce_two"):
        half = width // 2
        size = 8 * keep

        def gather(parts, axis):
            got = [shift(v, axis, 4, k) for v, k in zip(parts[:3], HOPS)]
            return parts[3] + sum(g.astype(f32) for g in got)

        one, two = gather(parts[:4], "x"), gather(parts[4:], "y")
        cut = lambda v: [v[i * size : (i + 1) * size] for i in range(3)]
        one = gather(cut(one.astype(bf16)) + [one[3 * size :]], "y")
        two = gather(cut(with_mass_columns(two, half)) + [two[3 * size :]], "x")
        part = wide = jnp.concatenate([one, two], axis=1)
        part = jnp.sum(swap(part, ("zh", "zl")).reshape(8, keep, width + 128), axis=0)
        mass = part[:, width : width + 1] + part[:, width + 1 : width + 2]
    with jax.named_scope("out_one"):
        mine = [
            lax.dynamic_index_in_dim(r.reshape(block, 2, 4, 2, width // 16), core, 3, False)
            for r in (rows, rows_other)
        ]
        both = jnp.where(core == 0, jnp.stack(mine), jnp.stack(mine[::-1]))
        both = both.transpose(2, 3, 0, 1, 4)
        stay = lax.dynamic_index_in_dim(both, zh, 0, False)
        go = lax.dynamic_index_in_dim(both, 1 - zh, 0, False)
        come = lax.ppermute(go, "zh", [(0, 1), (1, 0)])
        pair = jnp.where(zh == 0, jnp.stack([stay, come]), jnp.stack([come, stay]))
        pair = pair.transpose(1, 0, 2, 3, 4)
        by_x = [lax.dynamic_index_in_dim(pair, (x + k) % 4, 0, False) for k in range(4)]
        by_x, _ = lax.optimization_barrier((by_x, wide))
        by_x = jnp.stack([by_x[0]] + [shift(by_x[k], "x", 4, k) for k in (1, 2, 3)])
        by_x = jnp.roll(by_x[::-1], x + 1, axis=0)
        new_one = by_x.transpose(2, 0, 1, 3, 4).reshape(16 * block, width // 16)
    with jax.named_scope("finish_two"):
        place = lax.axis_index(ALL)
        old = lax.dynamic_slice_in_dim(cent_two, place * keep, keep, 0).astype(f32)
        new_two = ((part[:, :width] + prior_two * old) / (mass + prior_two)).astype(bf16)
    return (new_one, new_two)


def solution(mesh):
    inner = Mesh(mesh.devices.reshape(2, 4, 2, 4, 4), ALL)
    dp = ("zh", "x", "core")
    in_specs = (P(dp, None), P(CENT, None), P())
    out_specs = (P(CENT, dp), P(ALL, None))
    return jax.shard_map(
        on_device, mesh=inner, in_specs=in_specs, out_specs=out_specs, check_vma=False
    )
```

profile of v0, /device:TPU:8, one launch (start us, length us, event | category | flops | bytes accessed | tf_op | source)
XLA Modules:
  0.0 137.8 jit_solution(15172167806090223220)
XLA Ops:
  0.7 2.1 %multiply_reduce_fusion = f32[1024]{0:T(1024)S(1)} fusion(bf16[2048,1024]{1,0:T(8,128)(2,1)} %param.7, s32[]{:T(128)S(6)} %select_n.114), kind=kLoop, calls=%fused_computation.4 | loop fusion | flops 3144704 | bytes 2101252 | tf_op jit(solution)/shard_map/scores_one/reduce_sum | solution.py:238
  2.8 4.6 %fusion.4 = (f32[1024]{0:T(1024)S(1)}, f32[1024,1024]{1,0:T(8,128)S(1)}) fusion(f32[1024]{0:T(1024)S(1)} %multiply_reduce_fusion, bf16[1024,1024]{1,0:T(8,128)(2,1)} %p_mine.3, bf16[2048,1024]{1,0:T(8,128)(2,1)} %param.7, s32[]{:T(128)S(6)} %select_n.114), kind=kOutput, calls=%fused_computation.9 | convolution fusion | flops 2151676928 | bytes 8396804 | tf_op jit(solution)/shard_map/scores_one/dot_general | solution.py:37
  7.5 2.4 %fusion = (f32[1024]{0:T(1024)S(1)}, bf16[1024,1024]{1,0:T(8,128)(2,1)}) fusion(f32[1024,1024]{1,0:T(8,128)S(1)} %get-tuple-element.82, f32[1024]{0:T(1024)S(1)} %get-tuple-element.28, f32[1024]{0:T(1024)S(1)} %multiply_reduce_fusion), kind=kLoop, calls=%fused_computation.5 | loop fusion | flops 6290432 | bytes 6303744 | tf_op jit(solution)/shard_map/scores_one/reduce_sum | solution.py:244
  10.0 2.4 %fusion.5 = (f32[1024]{0:T(1024)S(1)}, f32[1024,1024]{1,0:T(8,128)S(1)}) fusion(f32[1024]{0:T(1024)S(1)} %multiply_reduce_fusion, bf16[1024,1024]{1,0:T(8,128)(2,1)S(1)} %collective-permute-done.p_other, bf16[2048,1024]{1,0:T(8,128)(2,1)S(1)} %copy-done.1, s32[]{:T(128)S(6)} %select_n.114), kind=kOutput, calls=%fused_computation.10 | convolution fusion | flops 2151676928 | bytes 8396804 | tf_op jit(solution)/shard_map/scores_one/dot_general | solution.py:37
  12.5 2.4 %fusion.2 = (f32[1024]{0:T(1024)S(1)}, bf16[1024,1024]{1,0:T(8,128)(2,1)}) fusion(f32[1024,1024]{1,0:T(8,128)S(1)} %get-tuple-element.84, f32[1024]{0:T(1024)S(1)} %get-tuple-element.83, f32[1024]{0:T(1024)S(1)} %multiply_reduce_fusion), kind=kLoop, calls=%fused_computation.7 | loop fusion | flops 6290432 | bytes 6303744 | tf_op jit(solution)/shard_map/scores_one/reduce_sum | solution.py:244
  16.9 9.0 %all-to-all-start = ((f32[16,1,1024]{2,1,0:T(1,128)}), f32[16,1,1024]{2,1,0:T(1,128)S(1)}, u32[]{:S(2)}, u32[]{:S(2)}) async-start(f32[16,1,1024]{2,1,0:T(1,128)} %broadcast_in_dim.49), calls=%async_computation | async-start | bytes 131072 | tf_op jit(solution)/shard_map/exchange_softmax/all_to_all | solution.py:25
  25.9 7.0 %all-to-all-done = f32[16,1,1024]{2,1,0:T(1,128)S(1)} async-done(((f32[16,1,1024]{2,1,0:T(1,128)}), f32[16,1,1024]{2,1,0:T(1,128)S(1)}, u32[]{:S(2)}, u32[]{:S(2)}) %all-to-all-start) | async-done | bytes 65568 | tf_op jit(solution)/shard_map/exchange_softmax/all_to_all | solution.py:25
  34.3 6.5 %level_one_sums.3 = (bf16[144,1024]{1,0:T(8,128)(2,1)S(1)}, bf16[144,1024]{1,0:T(8,128)(2,1)S(1)}, bf16[144,1024]{1,0:T(8,128)(2,1)S(1)}, f32[144,1024]{1,0:T(8,128)S(1)}) custom-call(s32[4]{0:T(128)S(1)} %multiply_add_fusion.index, bf16[1024,1024]{1,0:T(8,128)(2,1)} %get-tuple-element.26.e_mine, bf16[1024,1024]{1,0:T(8,128)(2,1)} %get-tuple-element.61.e_other, ...), custom_call_target="tpu_custom_call" | custom-call | flops 2147483648 | bytes 8388608 | tf_op jit(solution)/shard_map/reduce_one/level_one_sums/pallas_call | solution.py:118
  40.8 3.1 %collective-permute-start.6 = (bf16[144,1024]{1,0:T(8,128)(2,1)S(1)}, bf16[144,1024]{1,0:T(8,128)(2,1)S(1)}, u32[]{:S(2)}, u32[]{:S(2)}) collective-permute-start(bf16[144,1024]{1,0:T(8,128)(2,1)S(1)} %get-tuple-element.35), channel_id=1, source_target_pairs={{0,64},{32,96},{64,0},{96,32},{1,65},{33,97},{65,1},{97,33},{2,66}... | collective-permute-start | bytes 884744 | tf_op jit(solution)/shard_map/reduce_one/ppermute | solution.py:29
  44.5 2.6 %collective-permute-start.8 = (bf16[144,1024]{1,0:T(8,128)(2,1)S(1)}, bf16[144,1024]{1,0:T(8,128)(2,1)S(1)}, u32[]{:S(2)}, u32[]{:S(2)}) collective-permute-start(bf16[144,1024]{1,0:T(8,128)(2,1)S(1)} %get-tuple-element.37), channel_id=1, source_target_pairs={{0,96},{32,0},{64,32},{96,64},{1,97},{33,1},{65,33},{97,65},{2,98}... | collective-permute-start | bytes 884744 | tf_op jit(solution)/shard_map/reduce_one/ppermute | solution.py:29
  47.1 6.5 %level_one_sums.2 = (bf16[144,1024]{1,0:T(8,128)(2,1)S(1)}, bf16[144,1024]{1,0:T(8,128)(2,1)S(1)}, bf16[144,1024]{1,0:T(8,128)(2,1)S(1)}, f32[144,1024]{1,0:T(8,128)S(1)}) custom-call(s32[4]{0:T(128)S(1)} %get-tuple-element.56.index, bf16[1024,1024]{1,0:T(8,128)(2,1)} %get-tuple-element.26.e_mine, bf16[1024,1024]{1,0:T(8,128)(2,1)} %get-tuple-element.61.e_other, ...), custom_call_target="tpu_custom_call" | custom-call | flops 2147483648 | bytes 8388608 | tf_op jit(solution)/shard_map/reduce_one/level_one_sums/pallas_call | solution.py:118
  54.6 2.5 %collective-permute-start.5 = (bf16[144,1024]{1,0:T(8,128)(2,1)S(1)}, bf16[144,1024]{1,0:T(8,128)(2,1)S(1)}, u32[]{:S(2)}, u32[]{:S(2)}) collective-permute-start(bf16[144,1024]{1,0:T(8,128)(2,1)S(1)} %get-tuple-element.33), channel_id=1, source_target_pairs={{0,96},{32,0},{64,32},{96,64},{1,97},{33,1},{65,33},{97,65},{2,98}... | collective-permute-start | bytes 884744 | tf_op jit(solution)/shard_map/reduce_one/ppermute | solution.py:29
  57.0 1.5 %collective-permute-done.7 = bf16[144,1024]{1,0:T(8,128)(2,1)S(1)} collective-permute-done((bf16[144,1024]{1,0:T(8,128)(2,1)S(1)}, bf16[144,1024]{1,0:T(8,128)(2,1)S(1)}, u32[]{:S(2)}, u32[]{:S(2)}) %collective-permute-start.7) | collective-permute-done | bytes 294944 | tf_op jit(solution)/shard_map/reduce_one/ppermute | solution.py:29
  59.0 4.6 %collective-permute-start.9 = (bf16[144,1024]{1,0:T(8,128)(2,1)S(1)}, bf16[144,1024]{1,0:T(8,128)(2,1)S(1)}, u32[]{:S(2)}, u32[]{:S(2)}) collective-permute-start(bf16[144,1024]{1,0:T(8,128)(2,1)S(1)} %select_convert_fusion.1), channel_id=1, source_target_pairs={{0,128},{128,0},{1,129},{129,1},{2,130},{130,2},{3,131},{131,3},{4... | collective-permute-start | bytes 884744 | tf_op jit(solution)/shard_map/reduce_one/ppermute | solution.py:262
  63.6 1.6 %collective-permute-done.3 = bf16[144,1024]{1,0:T(8,128)(2,1)S(1)} collective-permute-done((bf16[144,1024]{1,0:T(8,128)(2,1)S(1)}, bf16[144,1024]{1,0:T(8,128)(2,1)S(1)}, u32[]{:S(2)}, u32[]{:S(2)}) %collective-permute-start.3) | collective-permute-done | bytes 294944 | tf_op jit(solution)/shard_map/reduce_one/ppermute | solution.py:29
  65.2 5.2 %collective-permute-done.4 = bf16[144,1024]{1,0:T(8,128)(2,1)S(1)} collective-permute-done((bf16[144,1024]{1,0:T(8,128)(2,1)S(1)}, bf16[144,1024]{1,0:T(8,128)(2,1)S(1)}, u32[]{:S(2)}, u32[]{:S(2)}) %collective-permute-start.4) | collective-permute-done | bytes 294944 | tf_op jit(solution)/shard_map/reduce_one/ppermute | solution.py:29
  70.6 7.3 %collective-permute-done.9 = bf16[144,1024]{1,0:T(8,128)(2,1)S(1)} collective-permute-done((bf16[144,1024]{1,0:T(8,128)(2,1)S(1)}, bf16[144,1024]{1,0:T(8,128)(2,1)S(1)}, u32[]{:S(2)}, u32[]{:S(2)}) %collective-permute-start.9) | collective-permute-done | bytes 294944 | tf_op jit(solution)/shard_map/reduce_one/ppermute | solution.py:262
  81.0 4.9 %level_two_sums.1 = (bf16[256,512]{1,0:T(8,128)(2,1)S(1)}, bf16[256,512]{1,0:T(8,128)(2,1)S(1)}, bf16[256,512]{1,0:T(8,128)(2,1)S(1)}, f32[256,512]{1,0:T(8,128)...) custom-call(s32[9]{0:T(128)S(1)} %pad_add_fusion.place, ...), custom_call_target="tpu_custom_call" | custom-call | flops 2147483648 | bytes 8388608 | tf_op jit(solution)/shard_map/scores_two/level_two_sums/pallas_call | solution.py:201
  87.0 2.7 %collective-permute-start.14 = (bf16[256,512]{1,0:T(8,128)(2,1)S(1)}, bf16[256,512]{1,0:T(8,128)(2,1)}, u32[]{:S(2)}, u32[]{:S(2)}) collective-permute-start(bf16[256,512]{1,0:T(8,128)(2,1)S(1)} %get-tuple-element.40), channel_id=1, source_target_pairs={{0,32},{32,64},{64,96},{96,0},{1,33},{33,65},{65,97},{97,1},{2,34}... | collective-permute-start | bytes 786440 | tf_op jit(solution)/shard_map/reduce_two/ppermute | solution.py:29
  90.4 2.9 %collective-permute-start.20 = (bf16[256,640]{1,0:T(8,128)(2,1)S(1)}, bf16[256,640]{1,0:T(8,128)(2,1)}, u32[]{:S(2)}, u32[]{:S(2)}) collective-permute-start(bf16[256,640]{1,0:T(8,128)(2,1)S(1)} %get-tuple-element.44), channel_id=1, source_target_pairs={{0,1},{1,2},{2,3},{3,0},{4,5},{5,6},{6,7},{7,4},{8,9},{9,10},{10,1... | collective-permute-start | bytes 983048 | tf_op jit(solution)/shard_map/reduce_two/ppermute | solution.py:29
  95.1 1.6 %collective-permute-done.13 = bf16[256,512]{1,0:T(8,128)(2,1)} collective-permute-done((bf16[256,512]{1,0:T(8,128)(2,1)S(1)}, bf16[256,512]{1,0:T(8,128)(2,1)}, u32[]{:S(2)}, u32[]{:S(2)}) %collective-permute-start.13) | collective-permute-done | bytes 262176 | tf_op jit(solution)/shard_map/reduce_two/ppermute | solution.py:29
  96.8 1.5 %collective-permute-start.21 = (bf16[256,640]{1,0:T(8,128)(2,1)S(1)}, bf16[256,640]{1,0:T(8,128)(2,1)S(1)}, u32[]{:S(2)}, u32[]{:S(2)}) collective-permute-start(bf16[256,640]{1,0:T(8,128)(2,1)S(1)} %get-tuple-element.45), channel_id=1, source_target_pairs={{0,3},{1,0},{2,1},{3,2},{4,7},{5,4},{6,5},{7,6},{8,11},{9,8},{10,9... | collective-permute-start | bytes 983048 | tf_op jit(solution)/shard_map/reduce_two/ppermute | solution.py:29
  98.3 3.5 %collective-permute-done.14 = bf16[256,512]{1,0:T(8,128)(2,1)} collective-permute-done((bf16[256,512]{1,0:T(8,128)(2,1)S(1)}, bf16[256,512]{1,0:T(8,128)(2,1)}, u32[]{:S(2)}, u32[]{:S(2)}) %collective-permute-start.14) | collective-permute-done | bytes 262176 | tf_op jit(solution)/shard_map/reduce_two/ppermute | solution.py:29
  101.7 3.2 %collective-permute-start.11 = (bf16[4,2,128,64]{2,3,0,1:T(8,128)(2,1)}, bf16[4,2,128,64]{2,3,0,1:T(8,128)(2,1)S(1)}, u32[]{:S(2)}, u32[]{:S(2)}) collective-permute-start(bf16[4,2,128,64]{2,3,0,1:T(8,128)(2,1)} %get-tuple-element.79), channel_id=1, source_target_pairs={{0,128},{128,0},{1,129},{129,1},{2,130},{130,2},{3,131},{131,3},{4... | collective-permute-start | bytes 393224 | tf_op jit(solution)/shard_map/out_one/ppermute | solution.py:299
  106.2 1.9 %collective-permute-start.16 = (bf16[64,512]{1,0:T(8,128)(2,1)S(1)}, bf16[64,512]{1,0:T(8,128)(2,1)S(1)}, u32[]{:S(2)}, u32[]{:S(2)}) collective-permute-start(bf16[64,512]{1,0:T(8,128)(2,1)S(1)} %get-tuple-element.71), channel_id=1, source_target_pairs={{0,2},{1,3},{2,0},{3,1},{4,6},{5,7},{6,4},{7,5},{8,10},{9,11},{10,... | collective-permute-start | bytes 196616 | tf_op jit(solution)/shard_map/reduce_two/ppermute | solution.py:29
  113.8 2.3 %collective-permute-start.24 = (bf16[64,640]{1,0:T(8,128)(2,1)S(1)}, bf16[64,640]{1,0:T(8,128)(2,1)S(1)}, u32[]{:S(2)}, u32[]{:S(2)}) collective-permute-start(bf16[64,640]{1,0:T(8,128)(2,1)S(1)} %get-tuple-element.69), channel_id=1, source_target_pairs={{0,96},{32,0},{64,32},{96,64},{1,97},{33,1},{65,33},{97,65},{2,98}... | collective-permute-start | bytes 245768 | tf_op jit(solution)/shard_map/reduce_two/ppermute | solution.py:29
  116.1 1.9 %collective-permute-done.22 = bf16[64,640]{1,0:T(8,128)(2,1)S(1)} collective-permute-done((bf16[64,640]{1,0:T(8,128)(2,1)S(1)}, bf16[64,640]{1,0:T(8,128)(2,1)S(1)}, u32[]{:S(2)}, u32[]{:S(2)}) %collective-permute-start.22) | collective-permute-done | bytes 81952 | tf_op jit(solution)/shard_map/reduce_two/ppermute | solution.py:29
  119.6 4.5 %all-to-all-start.1 = ((f32[8,8,1152]{2,1,0:T(8,128)}), f32[8,8,1152]{2,1,0:T(8,128)S(1)}, u32[]{:S(2)}, u32[]{:S(2)}) async-start(f32[8,8,1152]{2,1,0:T(8,128)} %fusion.28), calls=%async_computation.1 | async-start | bytes 589824 | tf_op jit(solution)/shard_map/reduce_two/all_to_all | solution.py:25
  125.6 3.2 %collective-permute-start.26 = (bf16[2,2,128,64]{2,3,1,0:T(8,128)(2,1)S(1)}, bf16[2,2,128,64]{2,3,1,0:T(8,128)(2,1)S(1)}, u32[]{:S(2)}, u32[]{:S(2)}) collective-permute-start(bf16[2,2,128,64]{2,3,1,0:T(8,128)(2,1)S(1)} %get-tuple-element.48), channel_id=1, source_target_pairs={{0,64},{32,96},{64,0},{96,32},{1,65},{33,97},{65,1},{97,33},{2,66}... | collective-permute-start | bytes 196616 | tf_op jit(solution)/shard_map/out_one/ppermute | solution.py:29
  129.8 1.9 %collective-permute-done.26 = bf16[2,2,128,64]{2,3,1,0:T(8,128)(2,1)S(1)} collective-permute-done((bf16[2,2,128,64]{2,3,1,0:T(8,128)(2,1)S(1)}, bf16[2,2,128,64]{2,3,1,0:T(8,128)(2,1)S(1)}, u32[]{:S(2)}, u32[]{:S(2)}) %collective-permute-start.26) | collective-permute-done | bytes 65568 | tf_op jit(solution)/shard_map/out_one/ppermute | solution.py:29
  134.4 1.8 %all-to-all-done.1 = f32[8,8,1152]{2,1,0:T(8,128)S(1)} async-done(((f32[8,8,1152]{2,1,0:T(8,128)}), f32[8,8,1152]{2,1,0:T(8,128)S(1)}, u32[]{:S(2)}, u32[]{:S(2)}) %all-to-all-start.1) | async-done | bytes 294944 | tf_op jit(solution)/shard_map/reduce_two/all_to_all | solution.py:25
  136.4 1.4 %fusion.18 = bf16[8,1024]{1,0:T(8,128)(2,1)} fusion(f32[8,1152]{1,0:T(8,128)S(1)} %reduce_sum.59, f32[8]{0:T(128)S(1)} %fusion.22, bf16[2048,1024]{1,0:T(8,128)(2,1)} %table_far.1, s32[]{:T(128)S(6)} %select_n.137), kind=kLoop, calls=%fused_computation.51 | loop fusion | flops 40960 | bytes 65572 | tf_op jit(solution)/shard_map/finish_two/convert_element_type | solution.py:310
  (90 shorter events, 26.3 us)
Async XLA Ops:
  0.6 9.3 %collective-permute-start = (bf16[1024,1024]{1,0:T(8,128)(2,1)}, bf16[1024,1024]{1,0:T(8,128)(2,1)S(1)}, u32[]{:S(2)}, u32[]{:S(2)}) collective-permute-start(bf16[1024,1024]{1,0:T(8,128)(2,1)} %p_mine.3), channel_id=1, source_target_pairs={{0,16},{16,0},{1,17},{17,1},{2,18},{18,2},{3,19},{19,3},{4,20},{20... | collective-permute-start | bytes 6291464 | tf_op jit(solution)/shard_map/scores_one/ppermute | solution.py:29
  7.4 2.6 %copy-start.1 = (bf16[2048,1024]{1,0:T(8,128)(2,1)S(1)}, bf16[2048,1024]{1,0:T(8,128)(2,1)}, u32[]{:S(2)}) copy-start(bf16[2048,1024]{1,0:T(8,128)(2,1)} %param.7) | copy-start | bytes 12582916
  12.5 13.4 %copy-start.2 = (s32[4]{0:T(128)S(1)}, s32[4]{0:T(128)}, u32[]{:S(2)}) copy-start(s32[4]{0:T(128)} %constant.146.clone) | copy-start | bytes 52
  14.9 1.3 collective-permute-start.1
  16.9 16.0 %all-to-all-start = ((f32[16,1,1024]{2,1,0:T(1,128)}), f32[16,1,1024]{2,1,0:T(1,128)S(1)}, u32[]{:S(2)}, u32[]{:S(2)}) async-start(f32[16,1,1024]{2,1,0:T(1,128)} %broadcast_in_dim.49), calls=%async_computation | async-start | bytes 131072 | tf_op jit(solution)/shard_map/exchange_softmax/all_to_all | solution.py:25
  33.0 1.3 collective-permute-start.2
  40.8 13.8 %collective-permute-start.6 = (bf16[144,1024]{1,0:T(8,128)(2,1)S(1)}, bf16[144,1024]{1,0:T(8,128)(2,1)S(1)}, u32[]{:S(2)}, u32[]{:S(2)}) collective-permute-start(bf16[144,1024]{1,0:T(8,128)(2,1)S(1)} %get-tuple-element.35), channel_id=1, source_target_pairs={{0,64},{32,96},{64,0},{96,32},{1,65},{33,97},{65,1},{97,33},{2,66}... | collective-permute-start | bytes 884744 | tf_op jit(solution)/shard_map/reduce_one/ppermute | solution.py:29
  43.9 14.6 %collective-permute-start.7 = (bf16[144,1024]{1,0:T(8,128)(2,1)S(1)}, bf16[144,1024]{1,0:T(8,128)(2,1)S(1)}, u32[]{:S(2)}, u32[]{:S(2)}) collective-permute-start(bf16[144,1024]{1,0:T(8,128)(2,1)S(1)} %get-tuple-element.36), channel_id=1, source_target_pairs={{0,32},{32,64},{64,96},{96,0},{1,33},{33,65},{65,97},{97,1},{2,34}... | collective-permute-start | bytes 884744 | tf_op jit(solution)/shard_map/reduce_one/ppermute | solution.py:29
  44.5 14.2 %collective-permute-start.8 = (bf16[144,1024]{1,0:T(8,128)(2,1)S(1)}, bf16[144,1024]{1,0:T(8,128)(2,1)S(1)}, u32[]{:S(2)}, u32[]{:S(2)}) collective-permute-start(bf16[144,1024]{1,0:T(8,128)(2,1)S(1)} %get-tuple-element.37), channel_id=1, source_target_pairs={{0,96},{32,0},{64,32},{96,64},{1,97},{33,1},{65,33},{97,65},{2,98}... | collective-permute-start | bytes 884744 | tf_op jit(solution)/shard_map/reduce_one/ppermute | solution.py:29
  53.6 11.6 %collective-permute-start.3 = (bf16[144,1024]{1,0:T(8,128)(2,1)S(1)}, bf16[144,1024]{1,0:T(8,128)(2,1)S(1)}, u32[]{:S(2)}, u32[]{:S(2)}) collective-permute-start(bf16[144,1024]{1,0:T(8,128)(2,1)S(1)} %get-tuple-element.31), channel_id=1, source_target_pairs={{0,64},{32,96},{64,0},{96,32},{1,65},{33,97},{65,1},{97,33},{2,66}... | collective-permute-start | bytes 884744 | tf_op jit(solution)/shard_map/reduce_one/ppermute | solution.py:29
  53.7 16.7 %collective-permute-start.4 = (bf16[144,1024]{1,0:T(8,128)(2,1)S(1)}, bf16[144,1024]{1,0:T(8,128)(2,1)S(1)}, u32[]{:S(2)}, u32[]{:S(2)}) collective-permute-start(bf16[144,1024]{1,0:T(8,128)(2,1)S(1)} %get-tuple-element.32), channel_id=1, source_target_pairs={{0,32},{32,64},{64,96},{96,0},{1,33},{33,65},{65,97},{97,1},{2,34}... | collective-permute-start | bytes 884744 | tf_op jit(solution)/shard_map/reduce_one/ppermute | solution.py:29
  54.6 16.0 %collective-permute-start.5 = (bf16[144,1024]{1,0:T(8,128)(2,1)S(1)}, bf16[144,1024]{1,0:T(8,128)(2,1)S(1)}, u32[]{:S(2)}, u32[]{:S(2)}) collective-permute-start(bf16[144,1024]{1,0:T(8,128)(2,1)S(1)} %get-tuple-element.33), channel_id=1, source_target_pairs={{0,96},{32,0},{64,32},{96,64},{1,97},{33,1},{65,33},{97,65},{2,98}... | collective-permute-start | bytes 884744 | tf_op jit(solution)/shard_map/reduce_one/ppermute | solution.py:29
  59.0 18.9 %collective-permute-start.9 = (bf16[144,1024]{1,0:T(8,128)(2,1)S(1)}, bf16[144,1024]{1,0:T(8,128)(2,1)S(1)}, u32[]{:S(2)}, u32[]{:S(2)}) collective-permute-start(bf16[144,1024]{1,0:T(8,128)(2,1)S(1)} %select_convert_fusion.1), channel_id=1, source_target_pairs={{0,128},{128,0},{1,129},{129,1},{2,130},{130,2},{3,131},{131,3},{4... | collective-permute-start | bytes 884744 | tf_op jit(solution)/shard_map/reduce_one/ppermute | solution.py:262
  79.2 1.8 %collective-permute-start.10 = (bf16[128,1024]{1,0:T(8,128)(2,1)S(1)}, bf16[128,1024]{1,0:T(8,128)(2,1)S(1)}, u32[]{:S(2)}, u32[]{:S(2)}) collective-permute-start(bf16[128,1024]{1,0:T(8,128)(2,1)S(1)} %fusion.11.rows_mine), channel_id=1, source_target_pairs={{0,16},{16,0},{1,17},{17,1},{2,18},{18,2},{3,19},{19,3},{4,20},{20... | collective-permute-start | bytes 786440 | tf_op jit(solution)/shard_map/finish_one/ppermute | solution.py:29
  79.6 1.4 %collective-permute-start.12 = (f32[128]{0:T(128)S(1)}, f32[128]{0:T(128)S(1)}, u32[]{:S(2)}, u32[]{:S(2)}) collective-permute-start(f32[128]{0:T(128)S(1)} %bitcast.68), channel_id=1, source_target_pairs={{0,16},{16,0},{1,17},{17,1},{2,18},{18,2},{3,19},{19,3},{4,20},{20... | collective-permute-start | bytes 1544 | tf_op jit(solution)/shard_map/finish_one/ppermute | solution.py:29
  85.9 10.9 %collective-permute-start.13 = (bf16[256,512]{1,0:T(8,128)(2,1)S(1)}, bf16[256,512]{1,0:T(8,128)(2,1)}, u32[]{:S(2)}, u32[]{:S(2)}) collective-permute-start(bf16[256,512]{1,0:T(8,128)(2,1)S(1)} %get-tuple-element.39), channel_id=1, source_target_pairs={{0,64},{32,96},{64,0},{96,32},{1,65},{33,97},{65,1},{97,33},{2,66}... | collective-permute-start | bytes 786440 | tf_op jit(solution)/shard_map/reduce_two/ppermute | solution.py:29
  87.0 14.7 %collective-permute-start.14 = (bf16[256,512]{1,0:T(8,128)(2,1)S(1)}, bf16[256,512]{1,0:T(8,128)(2,1)}, u32[]{:S(2)}, u32[]{:S(2)}) collective-permute-start(bf16[256,512]{1,0:T(8,128)(2,1)S(1)} %get-tuple-element.40), channel_id=1, source_target_pairs={{0,32},{32,64},{64,96},{96,0},{1,33},{33,65},{65,97},{97,1},{2,34}... | collective-permute-start | bytes 786440 | tf_op jit(solution)/shard_map/reduce_two/ppermute | solution.py:29
  89.7 15.2 %collective-permute-start.15 = (bf16[256,512]{1,0:T(8,128)(2,1)S(1)}, bf16[256,512]{1,0:T(8,128)(2,1)}, u32[]{:S(2)}, u32[]{:S(2)}) collective-permute-start(bf16[256,512]{1,0:T(8,128)(2,1)S(1)} %get-tuple-element.41), channel_id=1, source_target_pairs={{0,96},{32,0},{64,32},{96,64},{1,97},{33,1},{65,33},{97,65},{2,98}... | collective-permute-start | bytes 786440 | tf_op jit(solution)/shard_map/reduce_two/ppermute | solution.py:29
  90.3 17.8 %collective-permute-start.19 = (bf16[256,640]{1,0:T(8,128)(2,1)S(1)}, bf16[256,640]{1,0:T(8,128)(2,1)}, u32[]{:S(2)}, u32[]{:S(2)}) collective-permute-start(bf16[256,640]{1,0:T(8,128)(2,1)S(1)} %get-tuple-element.43), channel_id=1, source_target_pairs={{0,2},{1,3},{2,0},{3,1},{4,6},{5,7},{6,4},{7,5},{8,10},{9,11},{10,... | collective-permute-start | bytes 983048 | tf_op jit(solution)/shard_map/reduce_two/ppermute | solution.py:29
  90.4 19.1 %collective-permute-start.20 = (bf16[256,640]{1,0:T(8,128)(2,1)S(1)}, bf16[256,640]{1,0:T(8,128)(2,1)}, u32[]{:S(2)}, u32[]{:S(2)}) collective-permute-start(bf16[256,640]{1,0:T(8,128)(2,1)S(1)} %get-tuple-element.44), channel_id=1, source_target_pairs={{0,1},{1,2},{2,3},{3,0},{4,5},{5,6},{6,7},{7,4},{8,9},{9,10},{10,1... | collective-permute-start | bytes 983048 | tf_op jit(solution)/shard_map/reduce_two/ppermute | solution.py:29
  96.8 13.3 %collective-permute-start.21 = (bf16[256,640]{1,0:T(8,128)(2,1)S(1)}, bf16[256,640]{1,0:T(8,128)(2,1)S(1)}, u32[]{:S(2)}, u32[]{:S(2)}) collective-permute-start(bf16[256,640]{1,0:T(8,128)(2,1)S(1)} %get-tuple-element.45), channel_id=1, source_target_pairs={{0,3},{1,0},{2,1},{3,2},{4,7},{5,4},{6,5},{7,6},{8,11},{9,8},{10,9... | collective-permute-start | bytes 983048 | tf_op jit(solution)/shard_map/reduce_two/ppermute | solution.py:29
  101.7 22.4 %collective-permute-start.11 = (bf16[4,2,128,64]{2,3,0,1:T(8,128)(2,1)}, bf16[4,2,128,64]{2,3,0,1:T(8,128)(2,1)S(1)}, u32[]{:S(2)}, u32[]{:S(2)}) collective-permute-start(bf16[4,2,128,64]{2,3,0,1:T(8,128)(2,1)} %get-tuple-element.79), channel_id=1, source_target_pairs={{0,128},{128,0},{1,129},{129,1},{2,130},{130,2},{3,131},{131,3},{4... | collective-permute-start | bytes 393224 | tf_op jit(solution)/shard_map/out_one/ppermute | solution.py:299
  106.2 6.7 %collective-permute-start.16 = (bf16[64,512]{1,0:T(8,128)(2,1)S(1)}, bf16[64,512]{1,0:T(8,128)(2,1)S(1)}, u32[]{:S(2)}, u32[]{:S(2)}) collective-permute-start(bf16[64,512]{1,0:T(8,128)(2,1)S(1)} %get-tuple-element.71), channel_id=1, source_target_pairs={{0,2},{1,3},{2,0},{3,1},{4,6},{5,7},{6,4},{7,5},{8,10},{9,11},{10,... | collective-permute-start | bytes 196616 | tf_op jit(solution)/shard_map/reduce_two/ppermute | solution.py:29
  108.1 5.7 %collective-permute-start.17 = (bf16[64,512]{1,0:T(8,128)(2,1)S(1)}, bf16[64,512]{1,0:T(8,128)(2,1)S(1)}, u32[]{:S(2)}, u32[]{:S(2)}) collective-permute-start(bf16[64,512]{1,0:T(8,128)(2,1)S(1)} %get-tuple-element.73), channel_id=1, source_target_pairs={{0,1},{1,2},{2,3},{3,0},{4,5},{5,6},{6,7},{7,4},{8,9},{9,10},{10,1... | collective-permute-start | bytes 196616 | tf_op jit(solution)/shard_map/reduce_two/ppermute | solution.py:29
  109.5 6.6 %collective-permute-start.18 = (bf16[64,512]{1,0:T(8,128)(2,1)S(1)}, bf16[64,512]{1,0:T(8,128)(2,1)S(1)}, u32[]{:S(2)}, u32[]{:S(2)}) collective-permute-start(bf16[64,512]{1,0:T(8,128)(2,1)S(1)} %get-tuple-element.72), channel_id=1, source_target_pairs={{0,3},{1,0},{2,1},{3,2},{4,7},{5,4},{6,5},{7,6},{8,11},{9,8},{10,9... | collective-permute-start | bytes 196616 | tf_op jit(solution)/shard_map/reduce_two/ppermute | solution.py:29
  111.7 6.2 %collective-permute-start.22 = (bf16[64,640]{1,0:T(8,128)(2,1)S(1)}, bf16[64,640]{1,0:T(8,128)(2,1)S(1)}, u32[]{:S(2)}, u32[]{:S(2)}) collective-permute-start(bf16[64,640]{1,0:T(8,128)(2,1)S(1)} %get-tuple-element.68), channel_id=1, source_target_pairs={{0,64},{32,96},{64,0},{96,32},{1,65},{33,97},{65,1},{97,33},{2,66}... | collective-permute-start | bytes 245768 | tf_op jit(solution)/shard_map/reduce_two/ppermute | solution.py:29
  112.8 6.0 %collective-permute-start.23 = (bf16[64,640]{1,0:T(8,128)(2,1)S(1)}, bf16[64,640]{1,0:T(8,128)(2,1)S(1)}, u32[]{:S(2)}, u32[]{:S(2)}) collective-permute-start(bf16[64,640]{1,0:T(8,128)(2,1)S(1)} %get-tuple-element.70), channel_id=1, source_target_pairs={{0,32},{32,64},{64,96},{96,0},{1,33},{33,65},{65,97},{97,1},{2,34}... | collective-permute-start | bytes 245768 | tf_op jit(solution)/shard_map/reduce_two/ppermute | solution.py:29
  113.8 5.0 %collective-permute-start.24 = (bf16[64,640]{1,0:T(8,128)(2,1)S(1)}, bf16[64,640]{1,0:T(8,128)(2,1)S(1)}, u32[]{:S(2)}, u32[]{:S(2)}) collective-permute-start(bf16[64,640]{1,0:T(8,128)(2,1)S(1)} %get-tuple-element.69), channel_id=1, source_target_pairs={{0,96},{32,0},{64,32},{96,64},{1,97},{33,1},{65,33},{97,65},{2,98}... | collective-permute-start | bytes 245768 | tf_op jit(solution)/shard_map/reduce_two/ppermute | solution.py:29
  119.6 16.6 %all-to-all-start.1 = ((f32[8,8,1152]{2,1,0:T(8,128)}), f32[8,8,1152]{2,1,0:T(8,128)S(1)}, u32[]{:S(2)}, u32[]{:S(2)}) async-start(f32[8,8,1152]{2,1,0:T(8,128)} %fusion.28), calls=%async_computation.1 | async-start | bytes 589824 | tf_op jit(solution)/shard_map/reduce_two/all_to_all | solution.py:25
  124.2 5.6 %collective-permute-start.25 = (bf16[2,2,128,64]{2,3,1,0:T(8,128)(2,1)S(1)}, bf16[2,2,128,64]{2,3,1,0:T(8,128)(2,1)S(1)}, u32[]{:S(2)}, u32[]{:S(2)}) collective-permute-start(bf16[2,2,128,64]{2,3,1,0:T(8,128)(2,1)S(1)} %get-tuple-element.47), channel_id=1, source_target_pairs={{0,32},{32,64},{64,96},{96,0},{1,33},{33,65},{65,97},{97,1},{2,34}... | collective-permute-start | bytes 196616 | tf_op jit(solution)/shard_map/out_one/ppermute | solution.py:29
  125.6 6.1 %collective-permute-start.26 = (bf16[2,2,128,64]{2,3,1,0:T(8,128)(2,1)S(1)}, bf16[2,2,128,64]{2,3,1,0:T(8,128)(2,1)S(1)}, u32[]{:S(2)}, u32[]{:S(2)}) collective-permute-start(bf16[2,2,128,64]{2,3,1,0:T(8,128)(2,1)S(1)} %get-tuple-element.48), channel_id=1, source_target_pairs={{0,64},{32,96},{64,0},{96,32},{1,65},{33,97},{65,1},{97,33},{2,66}... | collective-permute-start | bytes 196616 | tf_op jit(solution)/shard_map/out_one/ppermute | solution.py:29
  128.8 4.3 %collective-permute-start.27 = (bf16[2,2,128,64]{2,3,1,0:T(8,128)(2,1)S(1)}, bf16[2,2,128,64]{2,3,1,0:T(8,128)(2,1)S(1)}, u32[]{:S(2)}, u32[]{:S(2)}) collective-permute-start(bf16[2,2,128,64]{2,3,1,0:T(8,128)(2,1)S(1)} %get-tuple-element.49), channel_id=1, source_target_pairs={{0,96},{32,0},{64,32},{96,64},{1,97},{33,1},{65,33},{97,65},{2,98}... | collective-permute-start | bytes 196616 | tf_op jit(solution)/shard_map/out_one/ppermute | solution.py:29
  (1 other events, 2.6 us)
where the time goes:
time: 138 us
  starting transfers between devices  54.7 us (40%)
  waiting for transfers between devices  38.3 us (28%)
  Pallas kernels  17.9 us (13%)
  other arithmetic  15.2 us (11%)
  matrix products  7.05 us (5%)
  local copies, waits for them, and re-layouts  3.75 us (3%)
    ppermute x26, starting transfers between devices, shift(): return lax.ppermute(v, axis, [(i, (i + k) % n) for i in range(n)])  33.4 us
    ppermute x26, waiting for transfers between devices, shift(): return lax.ppermute(v, axis, [(i, (i + k) % n) for i in range(n)])  22.1 us
    all_to_all x2, starting transfers between devices, swap(): return lax.all_to_all(v, axis, 0, 0, tiled=True)  13.5 us
    pallas_call x2, Pallas kernels, level_one_sums(): pl.pallas_call(sums_kernel, in_specs=[pl.BlockSpec(memory_space=pltpu.SME...  13 us
    all_to_all x2, waiting for transfers between devices, swap(): return lax.all_to_all(v, axis, 0, 0, tiled=True)  8.84 us
    ppermute x1, waiting for transfers between devices, on_device(): lax.ppermute(with_mass(sums[0], block), 'zh', [(0, 1), (1, 0)]).astype(f32)  7.32 us
    dot_general x2, matrix products, dot(): return lax.dot_general(a, b, (dims, ((), ())), preferred_element_type=f32)  7.05 us
    pallas_call x1, Pallas kernels, level_two_sums(): pl.pallas_call(functools.partial(level_two_kernel, count // 256), in_spec...  4.91 us
  transfers between devices with their start and end apart: 30, of which 18 were waited for; matrix products, arithmetic and copies ran while one was open for 13% of the time, Pallas kernels for 5%

commit v1 on v0

--- a/solution.py
+++ b/solution.py
@@ -66,14 +66,16 @@
         at = pl.ds(pl.multiple_of(index[i] * block, block), block)
         return pltpu.make_async_copy(e.at[at, :], e_held.at[j, i], e_sem.at[j, i])
 
-    p_copies = [
-        pltpu.make_async_copy(p, p_held.at[j], p_sem.at[j]) for j, p in enumerate((p_mine, p_other))
-    ]
+    def p_copy(n, j, p):
+        at = pl.ds(pl.multiple_of(n * (width // 4), width // 4), width // 4)
+        return pltpu.make_async_copy(p.at[:, at], p_held.at[j, :, at], p_sem.at[j, n])
+
     for i in range(4):
         for j, e in enumerate((e_mine, e_other)):
             e_copy(i, j, e).start()
-    for copy in p_copies:
-        copy.start()
+    for n in range(4):
+        for j, p in enumerate((p_mine, p_other)):
+            p_copy(n, j, p).start()
 
     def fill(i, carry):
         to = pl.ds(pl.multiple_of(i * block, block), block)
@@ -90,11 +92,11 @@
     lax.fori_loop(0, 4, fill, 0)
     mass = jnp.sum(lanes[...].T, axis=0, keepdims=True)
     line = lax.broadcasted_iota(jnp.int32, (EXTRA, block), 0)
-    for copy in p_copies:
-        copy.wait()
 
     def tile(n, carry):
         cols = pl.ds(pl.multiple_of(n * (width // 4), width // 4), width // 4)
+        for j, p in enumerate((p_mine, p_other)):
+            p_copy(n, j, p).wait()
         v = dot(weights[:, :count], p_held[0, :, cols], ((1,), (0,)))
         v += dot(weights[:, count:], p_held[1, :, cols], ((1,), (0,)))
         for i, ref in enumerate(outs):
@@ -125,7 +127,7 @@
             pltpu.VMEM((2, 4, block, count), bf16),
             pltpu.VMEM((2, count, width), bf16),
             pltpu.SemaphoreType.DMA((2, 4)),
-            pltpu.SemaphoreType.DMA((2,)),
+            pltpu.SemaphoreType.DMA((2, 4)),
         ],
         out_shape=[jax.ShapeDtypeStruct((block + EXTRA, width), t) for t in types],
         compiler_params=pltpu.CompilerParams(vmem_limit_bytes=VMEM),

time: 138 us -> 138 us (level)
  no operation moved by 1% of the time
where the time goes in v1:
time: 138 us
  starting transfers between devices  54.8 us (40%)
  waiting for transfers between devices  38.1 us (28%)
  Pallas kernels  17.9 us (13%)
  other arithmetic  15.2 us (11%)
  matrix products  7.05 us (5%)
  local copies, waits for them, and re-layouts  3.75 us (3%)
    ppermute x26, starting transfers between devices, shift(): return lax.ppermute(v, axis, [(i, (i + k) % n) for i in range(n)])  33.5 us
    ppermute x26, waiting for transfers between devices, shift(): return lax.ppermute(v, axis, [(i, (i + k) % n) for i in range(n)])  22 us
    all_to_all x2, starting transfers between devices, swap(): return lax.all_to_all(v, axis, 0, 0, tiled=True)  13.5 us
    pallas_call x2, Pallas kernels, level_one_sums(): pl.pallas_call(sums_kernel, in_specs=[pl.BlockSpec(memory_space=pltpu.SME...  13 us
    all_to_all x2, waiting for transfers between devices, swap(): return lax.all_to_all(v, axis, 0, 0, tiled=True)  8.84 us
    ppermute x1, waiting for transfers between devices, on_device(): lax.ppermute(with_mass(sums[0], block), 'zh', [(0, 1), (1, 0)]).astype(f32)  7.29 us
    dot_general x2, matrix products, dot(): return lax.dot_general(a, b, (dims, ((), ())), preferred_element_type=f32)  7.05 us
    pallas_call x1, Pallas kernels, level_two_sums(): pl.pallas_call(functools.partial(level_two_kernel, count // 256), in_spec...  4.91 us
  transfers between devices with their start and end apart: 30, of which 18 were waited for; matrix products, arithmetic and copies ran while one was open for 13% of the time, Pallas kernels for 5%

profile of v1, /device:TPU:8, one launch (start us, length us, event | category | flops | bytes accessed | tf_op | source)
XLA Modules:
  0.0 137.8 jit_solution(7842277565500886082)
XLA Ops:
  0.7 2.1 %multiply_reduce_fusion = f32[1024]{0:T(1024)S(1)} fusion(bf16[2048,1024]{1,0:T(8,128)(2,1)} %param.7, s32[]{:T(128)S(6)} %select_n.114), kind=kLoop, calls=%fused_computation.4 | loop fusion | flops 3144704 | bytes 2101252 | tf_op jit(solution)/shard_map/scores_one/reduce_sum | solution.py:240
  2.8 4.6 %fusion.4 = (f32[1024]{0:T(1024)S(1)}, f32[1024,1024]{1,0:T(8,128)S(1)}) fusion(f32[1024]{0:T(1024)S(1)} %multiply_reduce_fusion, bf16[1024,1024]{1,0:T(8,128)(2,1)} %p_mine.3, bf16[2048,1024]{1,0:T(8,128)(2,1)} %param.7, s32[]{:T(128)S(6)} %select_n.114), kind=kOutput, calls=%fused_computation.9 | convolution fusion | flops 2151676928 | bytes 8396804 | tf_op jit(solution)/shard_map/scores_one/dot_general | solution.py:37
  7.5 2.4 %fusion = (f32[1024]{0:T(1024)S(1)}, bf16[1024,1024]{1,0:T(8,128)(2,1)}) fusion(f32[1024,1024]{1,0:T(8,128)S(1)} %get-tuple-element.82, f32[1024]{0:T(1024)S(1)} %get-tuple-element.28, f32[1024]{0:T(1024)S(1)} %multiply_reduce_fusion), kind=kLoop, calls=%fused_computation.5 | loop fusion | flops 6290432 | bytes 6303744 | tf_op jit(solution)/shard_map/scores_one/reduce_sum | solution.py:246
  10.0 2.4 %fusion.5 = (f32[1024]{0:T(1024)S(1)}, f32[1024,1024]{1,0:T(8,128)S(1)}) fusion(f32[1024]{0:T(1024)S(1)} %multiply_reduce_fusion, bf16[1024,1024]{1,0:T(8,128)(2,1)S(1)} %collective-permute-done.p_other, bf16[2048,1024]{1,0:T(8,128)(2,1)S(1)} %copy-done.1, s32[]{:T(128)S(6)} %select_n.114), kind=kOutput, calls=%fused_computation.10 | convolution fusion | flops 2151676928 | bytes 8396804 | tf_op jit(solution)/shard_map/scores_one/dot_general | solution.py:37
  12.5 2.4 %fusion.2 = (f32[1024]{0:T(1024)S(1)}, bf16[1024,1024]{1,0:T(8,128)(2,1)}) fusion(f32[1024,1024]{1,0:T(8,128)S(1)} %get-tuple-element.84, f32[1024]{0:T(1024)S(1)} %get-tuple-element.83, f32[1024]{0:T(1024)S(1)} %multiply_reduce_fusion), kind=kLoop, calls=%fused_computation.7 | loop fusion | flops 6290432 | bytes 6303744 | tf_op jit(solution)/shard_map/scores_one/reduce_sum | solution.py:246
  16.9 9.0 %all-to-all-start = ((f32[16,1,1024]{2,1,0:T(1,128)}), f32[16,1,1024]{2,1,0:T(1,128)S(1)}, u32[]{:S(2)}, u32[]{:S(2)}) async-start(f32[16,1,1024]{2,1,0:T(1,128)} %broadcast_in_dim.49), calls=%async_computation | async-start | bytes 131072 | tf_op jit(solution)/shard_map/exchange_softmax/all_to_all | solution.py:25
  25.9 7.0 %all-to-all-done = f32[16,1,1024]{2,1,0:T(1,128)S(1)} async-done(((f32[16,1,1024]{2,1,0:T(1,128)}), f32[16,1,1024]{2,1,0:T(1,128)S(1)}, u32[]{:S(2)}, u32[]{:S(2)}) %all-to-all-start) | async-done | bytes 65568 | tf_op jit(solution)/shard_map/exchange_softmax/all_to_all | solution.py:25
  34.3 6.5 %level_one_sums.3 = (bf16[144,1024]{1,0:T(8,128)(2,1)S(1)}, bf16[144,1024]{1,0:T(8,128)(2,1)S(1)}, bf16[144,1024]{1,0:T(8,128)(2,1)S(1)}, f32[144,1024]{1,0:T(8,128)S(1)}) custom-call(s32[4]{0:T(128)S(1)} %multiply_add_fusion.index, bf16[1024,1024]{1,0:T(8,128)(2,1)} %get-tuple-element.26.e_mine, bf16[1024,1024]{1,0:T(8,128)(2,1)} %get-tuple-element.61.e_other, ...), custom_call_target="tpu_custom_call" | custom-call | flops 2147483648 | bytes 8388608 | tf_op jit(solution)/shard_map/reduce_one/level_one_sums/pallas_call | solution.py:120
  40.8 3.1 %collective-permute-start.6 = (bf16[144,1024]{1,0:T(8,128)(2,1)S(1)}, bf16[144,1024]{1,0:T(8,128)(2,1)S(1)}, u32[]{:S(2)}, u32[]{:S(2)}) collective-permute-start(bf16[144,1024]{1,0:T(8,128)(2,1)S(1)} %get-tuple-element.35), channel_id=1, source_target_pairs={{0,64},{32,96},{64,0},{96,32},{1,65},{33,97},{65,1},{97,33},{2,66}... | collective-permute-start | bytes 884744 | tf_op jit(solution)/shard_map/reduce_one/ppermute | solution.py:29
  44.5 2.6 %collective-permute-start.8 = (bf16[144,1024]{1,0:T(8,128)(2,1)S(1)}, bf16[144,1024]{1,0:T(8,128)(2,1)S(1)}, u32[]{:S(2)}, u32[]{:S(2)}) collective-permute-start(bf16[144,1024]{1,0:T(8,128)(2,1)S(1)} %get-tuple-element.37), channel_id=1, source_target_pairs={{0,96},{32,0},{64,32},{96,64},{1,97},{33,1},{65,33},{97,65},{2,98}... | collective-permute-start | bytes 884744 | tf_op jit(solution)/shard_map/reduce_one/ppermute | solution.py:29
  47.2 6.5 %level_one_sums.2 = (bf16[144,1024]{1,0:T(8,128)(2,1)S(1)}, bf16[144,1024]{1,0:T(8,128)(2,1)S(1)}, bf16[144,1024]{1,0:T(8,128)(2,1)S(1)}, f32[144,1024]{1,0:T(8,128)S(1)}) custom-call(s32[4]{0:T(128)S(1)} %get-tuple-element.56.index, bf16[1024,1024]{1,0:T(8,128)(2,1)} %get-tuple-element.26.e_mine, bf16[1024,1024]{1,0:T(8,128)(2,1)} %get-tuple-element.61.e_other, ...), custom_call_target="tpu_custom_call" | custom-call | flops 2147483648 | bytes 8388608 | tf_op jit(solution)/shard_map/reduce_one/level_one_sums/pallas_call | solution.py:120
  54.7 2.5 %collective-permute-start.5 = (bf16[144,1024]{1,0:T(8,128)(2,1)S(1)}, bf16[144,1024]{1,0:T(8,128)(2,1)S(1)}, u32[]{:S(2)}, u32[]{:S(2)}) collective-permute-start(bf16[144,1024]{1,0:T(8,128)(2,1)S(1)} %get-tuple-element.33), channel_id=1, source_target_pairs={{0,96},{32,0},{64,32},{96,64},{1,97},{33,1},{65,33},{97,65},{2,98}... | collective-permute-start | bytes 884744 | tf_op jit(solution)/shard_map/reduce_one/ppermute | solution.py:29
  57.1 1.4 %collective-permute-done.7 = bf16[144,1024]{1,0:T(8,128)(2,1)S(1)} collective-permute-done((bf16[144,1024]{1,0:T(8,128)(2,1)S(1)}, bf16[144,1024]{1,0:T(8,128)(2,1)S(1)}, u32[]{:S(2)}, u32[]{:S(2)}) %collective-permute-start.7) | collective-permute-done | bytes 294944 | tf_op jit(solution)/shard_map/reduce_one/ppermute | solution.py:29
  59.0 4.6 %collective-permute-start.9 = (bf16[144,1024]{1,0:T(8,128)(2,1)S(1)}, bf16[144,1024]{1,0:T(8,128)(2,1)S(1)}, u32[]{:S(2)}, u32[]{:S(2)}) collective-permute-start(bf16[144,1024]{1,0:T(8,128)(2,1)S(1)} %select_convert_fusion.1), channel_id=1, source_target_pairs={{0,128},{128,0},{1,129},{129,1},{2,130},{130,2},{3,131},{131,3},{4... | collective-permute-start | bytes 884744 | tf_op jit(solution)/shard_map/reduce_one/ppermute | solution.py:264
  63.6 1.7 %collective-permute-done.3 = bf16[144,1024]{1,0:T(8,128)(2,1)S(1)} collective-permute-done((bf16[144,1024]{1,0:T(8,128)(2,1)S(1)}, bf16[144,1024]{1,0:T(8,128)(2,1)S(1)}, u32[]{:S(2)}, u32[]{:S(2)}) %collective-permute-start.3) | collective-permute-done | bytes 294944 | tf_op jit(solution)/shard_map/reduce_one/ppermute | solution.py:29
  65.3 5.2 %collective-permute-done.4 = bf16[144,1024]{1,0:T(8,128)(2,1)S(1)} collective-permute-done((bf16[144,1024]{1,0:T(8,128)(2,1)S(1)}, bf16[144,1024]{1,0:T(8,128)(2,1)S(1)}, u32[]{:S(2)}, u32[]{:S(2)}) %collective-permute-start.4) | collective-permute-done | bytes 294944 | tf_op jit(solution)/shard_map/reduce_one/ppermute | solution.py:29
  70.6 7.3 %collective-permute-done.9 = bf16[144,1024]{1,0:T(8,128)(2,1)S(1)} collective-permute-done((bf16[144,1024]{1,0:T(8,128)(2,1)S(1)}, bf16[144,1024]{1,0:T(8,128)(2,1)S(1)}, u32[]{:S(2)}, u32[]{:S(2)}) %collective-permute-start.9) | collective-permute-done | bytes 294944 | tf_op jit(solution)/shard_map/reduce_one/ppermute | solution.py:264
  81.0 4.9 %level_two_sums.1 = (bf16[256,512]{1,0:T(8,128)(2,1)S(1)}, bf16[256,512]{1,0:T(8,128)(2,1)S(1)}, bf16[256,512]{1,0:T(8,128)(2,1)S(1)}, f32[256,512]{1,0:T(8,128)...) custom-call(s32[9]{0:T(128)S(1)} %pad_add_fusion.place, ...), custom_call_target="tpu_custom_call" | custom-call | flops 2147483648 | bytes 8388608 | tf_op jit(solution)/shard_map/scores_two/level_two_sums/pallas_call | solution.py:203
  87.0 2.8 %collective-permute-start.14 = (bf16[256,512]{1,0:T(8,128)(2,1)S(1)}, bf16[256,512]{1,0:T(8,128)(2,1)}, u32[]{:S(2)}, u32[]{:S(2)}) collective-permute-start(bf16[256,512]{1,0:T(8,128)(2,1)S(1)} %get-tuple-element.40), channel_id=1, source_target_pairs={{0,32},{32,64},{64,96},{96,0},{1,33},{33,65},{65,97},{97,1},{2,34}... | collective-permute-start | bytes 786440 | tf_op jit(solution)/shard_map/reduce_two/ppermute | solution.py:29
  90.4 2.9 %collective-permute-start.20 = (bf16[256,640]{1,0:T(8,128)(2,1)S(1)}, bf16[256,640]{1,0:T(8,128)(2,1)}, u32[]{:S(2)}, u32[]{:S(2)}) collective-permute-start(bf16[256,640]{1,0:T(8,128)(2,1)S(1)} %get-tuple-element.44), channel_id=1, source_target_pairs={{0,1},{1,2},{2,3},{3,0},{4,5},{5,6},{6,7},{7,4},{8,9},{9,10},{10,1... | collective-permute-start | bytes 983048 | tf_op jit(solution)/shard_map/reduce_two/ppermute | solution.py:29
  95.2 1.6 %collective-permute-done.13 = bf16[256,512]{1,0:T(8,128)(2,1)} collective-permute-done((bf16[256,512]{1,0:T(8,128)(2,1)S(1)}, bf16[256,512]{1,0:T(8,128)(2,1)}, u32[]{:S(2)}, u32[]{:S(2)}) %collective-permute-start.13) | collective-permute-done | bytes 262176 | tf_op jit(solution)/shard_map/reduce_two/ppermute | solution.py:29
  96.8 1.5 %collective-permute-start.21 = (bf16[256,640]{1,0:T(8,128)(2,1)S(1)}, bf16[256,640]{1,0:T(8,128)(2,1)S(1)}, u32[]{:S(2)}, u32[]{:S(2)}) collective-permute-start(bf16[256,640]{1,0:T(8,128)(2,1)S(1)} %get-tuple-element.45), channel_id=1, source_target_pairs={{0,3},{1,0},{2,1},{3,2},{4,7},{5,4},{6,5},{7,6},{8,11},{9,8},{10,9... | collective-permute-start | bytes 983048 | tf_op jit(solution)/shard_map/reduce_two/ppermute | solution.py:29
  98.3 3.5 %collective-permute-done.14 = bf16[256,512]{1,0:T(8,128)(2,1)} collective-permute-done((bf16[256,512]{1,0:T(8,128)(2,1)S(1)}, bf16[256,512]{1,0:T(8,128)(2,1)}, u32[]{:S(2)}, u32[]{:S(2)}) %collective-permute-start.14) | collective-permute-done | bytes 262176 | tf_op jit(solution)/shard_map/reduce_two/ppermute | solution.py:29
  101.7 3.2 %collective-permute-start.11 = (bf16[4,2,128,64]{2,3,0,1:T(8,128)(2,1)}, bf16[4,2,128,64]{2,3,0,1:T(8,128)(2,1)S(1)}, u32[]{:S(2)}, u32[]{:S(2)}) collective-permute-start(bf16[4,2,128,64]{2,3,0,1:T(8,128)(2,1)} %get-tuple-element.79), channel_id=1, source_target_pairs={{0,128},{128,0},{1,129},{129,1},{2,130},{130,2},{3,131},{131,3},{4... | collective-permute-start | bytes 393224 | tf_op jit(solution)/shard_map/out_one/ppermute | solution.py:301
  106.2 1.9 %collective-permute-start.16 = (bf16[64,512]{1,0:T(8,128)(2,1)S(1)}, bf16[64,512]{1,0:T(8,128)(2,1)S(1)}, u32[]{:S(2)}, u32[]{:S(2)}) collective-permute-start(bf16[64,512]{1,0:T(8,128)(2,1)S(1)} %get-tuple-element.71), channel_id=1, source_target_pairs={{0,2},{1,3},{2,0},{3,1},{4,6},{5,7},{6,4},{7,5},{8,10},{9,11},{10,... | collective-permute-start | bytes 196616 | tf_op jit(solution)/shard_map/reduce_two/ppermute | solution.py:29
  113.9 2.3 %collective-permute-start.24 = (bf16[64,640]{1,0:T(8,128)(2,1)S(1)}, bf16[64,640]{1,0:T(8,128)(2,1)S(1)}, u32[]{:S(2)}, u32[]{:S(2)}) collective-permute-start(bf16[64,640]{1,0:T(8,128)(2,1)S(1)} %get-tuple-element.69), channel_id=1, source_target_pairs={{0,96},{32,0},{64,32},{96,64},{1,97},{33,1},{65,33},{97,65},{2,98}... | collective-permute-start | bytes 245768 | tf_op jit(solution)/shard_map/reduce_two/ppermute | solution.py:29
  116.2 1.8 %collective-permute-done.22 = bf16[64,640]{1,0:T(8,128)(2,1)S(1)} collective-permute-done((bf16[64,640]{1,0:T(8,128)(2,1)S(1)}, bf16[64,640]{1,0:T(8,128)(2,1)S(1)}, u32[]{:S(2)}, u32[]{:S(2)}) %collective-permute-start.22) | collective-permute-done | bytes 81952 | tf_op jit(solution)/shard_map/reduce_two/ppermute | solution.py:29
  119.6 4.5 %all-to-all-start.1 = ((f32[8,8,1152]{2,1,0:T(8,128)}), f32[8,8,1152]{2,1,0:T(8,128)S(1)}, u32[]{:S(2)}, u32[]{:S(2)}) async-start(f32[8,8,1152]{2,1,0:T(8,128)} %fusion.28), calls=%async_computation.1 | async-start | bytes 589824 | tf_op jit(solution)/shard_map/reduce_two/all_to_all | solution.py:25
  125.6 3.2 %collective-permute-start.26 = (bf16[2,2,128,64]{2,3,1,0:T(8,128)(2,1)S(1)}, bf16[2,2,128,64]{2,3,1,0:T(8,128)(2,1)S(1)}, u32[]{:S(2)}, u32[]{:S(2)}) collective-permute-start(bf16[2,2,128,64]{2,3,1,0:T(8,128)(2,1)S(1)} %get-tuple-element.48), channel_id=1, source_target_pairs={{0,64},{32,96},{64,0},{96,32},{1,65},{33,97},{65,1},{97,33},{2,66}... | collective-permute-start | bytes 196616 | tf_op jit(solution)/shard_map/out_one/ppermute | solution.py:29
  129.8 1.9 %collective-permute-done.26 = bf16[2,2,128,64]{2,3,1,0:T(8,128)(2,1)S(1)} collective-permute-done((bf16[2,2,128,64]{2,3,1,0:T(8,128)(2,1)S(1)}, bf16[2,2,128,64]{2,3,1,0:T(8,128)(2,1)S(1)}, u32[]{:S(2)}, u32[]{:S(2)}) %collective-permute-start.26) | collective-permute-done | bytes 65568 | tf_op jit(solution)/shard_map/out_one/ppermute | solution.py:29
  134.4 1.8 %all-to-all-done.1 = f32[8,8,1152]{2,1,0:T(8,128)S(1)} async-done(((f32[8,8,1152]{2,1,0:T(8,128)}), f32[8,8,1152]{2,1,0:T(8,128)S(1)}, u32[]{:S(2)}, u32[]{:S(2)}) %all-to-all-start.1) | async-done | bytes 294944 | tf_op jit(solution)/shard_map/reduce_two/all_to_all | solution.py:25
  136.4 1.4 %fusion.18 = bf16[8,1024]{1,0:T(8,128)(2,1)} fusion(f32[8,1152]{1,0:T(8,128)S(1)} %reduce_sum.59, f32[8]{0:T(128)S(1)} %fusion.22, bf16[2048,1024]{1,0:T(8,128)(2,1)} %table_far.1, s32[]{:T(128)S(6)} %select_n.137), kind=kLoop, calls=%fused_computation.51 | loop fusion | flops 40960 | bytes 65572 | tf_op jit(solution)/shard_map/finish_two/convert_element_type | solution.py:312
  (90 shorter events, 26.4 us)
Async XLA Ops:
  0.6 9.3 %collective-permute-start = (bf16[1024,1024]{1,0:T(8,128)(2,1)}, bf16[1024,1024]{1,0:T(8,128)(2,1)S(1)}, u32[]{:S(2)}, u32[]{:S(2)}) collective-permute-start(bf16[1024,1024]{1,0:T(8,128)(2,1)} %p_mine.3), channel_id=1, source_target_pairs={{0,16},{16,0},{1,17},{17,1},{2,18},{18,2},{3,19},{19,3},{4,20},{20... | collective-permute-start | bytes 6291464 | tf_op jit(solution)/shard_map/scores_one/ppermute | solution.py:29
  7.4 2.6 %copy-start.1 = (bf16[2048,1024]{1,0:T(8,128)(2,1)S(1)}, bf16[2048,1024]{1,0:T(8,128)(2,1)}, u32[]{:S(2)}) copy-start(bf16[2048,1024]{1,0:T(8,128)(2,1)} %param.7) | copy-start | bytes 12582916
  12.5 13.4 %copy-start.2 = (s32[4]{0:T(128)S(1)}, s32[4]{0:T(128)}, u32[]{:S(2)}) copy-start(s32[4]{0:T(128)} %constant.146.clone) | copy-start | bytes 52
  14.9 1.3 collective-permute-start.1
  16.9 16.0 %all-to-all-start = ((f32[16,1,1024]{2,1,0:T(1,128)}), f32[16,1,1024]{2,1,0:T(1,128)S(1)}, u32[]{:S(2)}, u32[]{:S(2)}) async-start(f32[16,1,1024]{2,1,0:T(1,128)} %broadcast_in_dim.49), calls=%async_computation | async-start | bytes 131072 | tf_op jit(solution)/shard_map/exchange_softmax/all_to_all | solution.py:25
  33.0 1.3 collective-permute-start.2
  40.8 13.8 %collective-permute-start.6 = (bf16[144,1024]{1,0:T(8,128)(2,1)S(1)}, bf16[144,1024]{1,0:T(8,128)(2,1)S(1)}, u32[]{:S(2)}, u32[]{:S(2)}) collective-permute-start(bf16[144,1024]{1,0:T(8,128)(2,1)S(1)} %get-tuple-element.35), channel_id=1, source_target_pairs={{0,64},{32,96},{64,0},{96,32},{1,65},{33,97},{65,1},{97,33},{2,66}... | collective-permute-start | bytes 884744 | tf_op jit(solution)/shard_map/reduce_one/ppermute | solution.py:29
  43.9 14.6 %collective-permute-start.7 = (bf16[144,1024]{1,0:T(8,128)(2,1)S(1)}, bf16[144,1024]{1,0:T(8,128)(2,1)S(1)}, u32[]{:S(2)}, u32[]{:S(2)}) collective-permute-start(bf16[144,1024]{1,0:T(8,128)(2,1)S(1)} %get-tuple-element.36), channel_id=1, source_target_pairs={{0,32},{32,64},{64,96},{96,0},{1,33},{33,65},{65,97},{97,1},{2,34}... | collective-permute-start | bytes 884744 | tf_op jit(solution)/shard_map/reduce_one/ppermute | solution.py:29
  44.5 14.2 %collective-permute-start.8 = (bf16[144,1024]{1,0:T(8,128)(2,1)S(1)}, bf16[144,1024]{1,0:T(8,128)(2,1)S(1)}, u32[]{:S(2)}, u32[]{:S(2)}) collective-permute-start(bf16[144,1024]{1,0:T(8,128)(2,1)S(1)} %get-tuple-element.37), channel_id=1, source_target_pairs={{0,96},{32,0},{64,32},{96,64},{1,97},{33,1},{65,33},{97,65},{2,98}... | collective-permute-start | bytes 884744 | tf_op jit(solution)/shard_map/reduce_one/ppermute | solution.py:29
  53.7 11.6 %collective-permute-start.3 = (bf16[144,1024]{1,0:T(8,128)(2,1)S(1)}, bf16[144,1024]{1,0:T(8,128)(2,1)S(1)}, u32[]{:S(2)}, u32[]{:S(2)}) collective-permute-start(bf16[144,1024]{1,0:T(8,128)(2,1)S(1)} %get-tuple-element.31), channel_id=1, source_target_pairs={{0,64},{32,96},{64,0},{96,32},{1,65},{33,97},{65,1},{97,33},{2,66}... | collective-permute-start | bytes 884744 | tf_op jit(solution)/shard_map/reduce_one/ppermute | solution.py:29
  53.8 16.7 %collective-permute-start.4 = (bf16[144,1024]{1,0:T(8,128)(2,1)S(1)}, bf16[144,1024]{1,0:T(8,128)(2,1)S(1)}, u32[]{:S(2)}, u32[]{:S(2)}) collective-permute-start(bf16[144,1024]{1,0:T(8,128)(2,1)S(1)} %get-tuple-element.32), channel_id=1, source_target_pairs={{0,32},{32,64},{64,96},{96,0},{1,33},{33,65},{65,97},{97,1},{2,34}... | collective-permute-start | bytes 884744 | tf_op jit(solution)/shard_map/reduce_one/ppermute | solution.py:29
  54.7 16.0 %collective-permute-start.5 = (bf16[144,1024]{1,0:T(8,128)(2,1)S(1)}, bf16[144,1024]{1,0:T(8,128)(2,1)S(1)}, u32[]{:S(2)}, u32[]{:S(2)}) collective-permute-start(bf16[144,1024]{1,0:T(8,128)(2,1)S(1)} %get-tuple-element.33), channel_id=1, source_target_pairs={{0,96},{32,0},{64,32},{96,64},{1,97},{33,1},{65,33},{97,65},{2,98}... | collective-permute-start | bytes 884744 | tf_op jit(solution)/shard_map/reduce_one/ppermute | solution.py:29
  59.0 18.9 %collective-permute-start.9 = (bf16[144,1024]{1,0:T(8,128)(2,1)S(1)}, bf16[144,1024]{1,0:T(8,128)(2,1)S(1)}, u32[]{:S(2)}, u32[]{:S(2)}) collective-permute-start(bf16[144,1024]{1,0:T(8,128)(2,1)S(1)} %select_convert_fusion.1), channel_id=1, source_target_pairs={{0,128},{128,0},{1,129},{129,1},{2,130},{130,2},{3,131},{131,3},{4... | collective-permute-start | bytes 884744 | tf_op jit(solution)/shard_map/reduce_one/ppermute | solution.py:264
  79.2 1.8 %collective-permute-start.10 = (bf16[128,1024]{1,0:T(8,128)(2,1)S(1)}, bf16[128,1024]{1,0:T(8,128)(2,1)S(1)}, u32[]{:S(2)}, u32[]{:S(2)}) collective-permute-start(bf16[128,1024]{1,0:T(8,128)(2,1)S(1)} %fusion.11.rows_mine), channel_id=1, source_target_pairs={{0,16},{16,0},{1,17},{17,1},{2,18},{18,2},{3,19},{19,3},{4,20},{20... | collective-permute-start | bytes 786440 | tf_op jit(solution)/shard_map/finish_one/ppermute | solution.py:29
  79.6 1.4 %collective-permute-start.12 = (f32[128]{0:T(128)S(1)}, f32[128]{0:T(128)S(1)}, u32[]{:S(2)}, u32[]{:S(2)}) collective-permute-start(f32[128]{0:T(128)S(1)} %bitcast.68), channel_id=1, source_target_pairs={{0,16},{16,0},{1,17},{17,1},{2,18},{18,2},{3,19},{19,3},{4,20},{20... | collective-permute-start | bytes 1544 | tf_op jit(solution)/shard_map/finish_one/ppermute | solution.py:29
  85.9 10.9 %collective-permute-start.13 = (bf16[256,512]{1,0:T(8,128)(2,1)S(1)}, bf16[256,512]{1,0:T(8,128)(2,1)}, u32[]{:S(2)}, u32[]{:S(2)}) collective-permute-start(bf16[256,512]{1,0:T(8,128)(2,1)S(1)} %get-tuple-element.39), channel_id=1, source_target_pairs={{0,64},{32,96},{64,0},{96,32},{1,65},{33,97},{65,1},{97,33},{2,66}... | collective-permute-start | bytes 786440 | tf_op jit(solution)/shard_map/reduce_two/ppermute | solution.py:29
  87.0 14.7 %collective-permute-start.14 = (bf16[256,512]{1,0:T(8,128)(2,1)S(1)}, bf16[256,512]{1,0:T(8,128)(2,1)}, u32[]{:S(2)}, u32[]{:S(2)}) collective-permute-start(bf16[256,512]{1,0:T(8,128)(2,1)S(1)} %get-tuple-element.40), channel_id=1, source_target_pairs={{0,32},{32,64},{64,96},{96,0},{1,33},{33,65},{65,97},{97,1},{2,34}... | collective-permute-start | bytes 786440 | tf_op jit(solution)/shard_map/reduce_two/ppermute | solution.py:29
  89.8 15.1 %collective-permute-start.15 = (bf16[256,512]{1,0:T(8,128)(2,1)S(1)}, bf16[256,512]{1,0:T(8,128)(2,1)}, u32[]{:S(2)}, u32[]{:S(2)}) collective-permute-start(bf16[256,512]{1,0:T(8,128)(2,1)S(1)} %get-tuple-element.41), channel_id=1, source_target_pairs={{0,96},{32,0},{64,32},{96,64},{1,97},{33,1},{65,33},{97,65},{2,98}... | collective-permute-start | bytes 786440 | tf_op jit(solution)/shard_map/reduce_two/ppermute | solution.py:29
  90.3 17.8 %collective-permute-start.19 = (bf16[256,640]{1,0:T(8,128)(2,1)S(1)}, bf16[256,640]{1,0:T(8,128)(2,1)}, u32[]{:S(2)}, u32[]{:S(2)}) collective-permute-start(bf16[256,640]{1,0:T(8,128)(2,1)S(1)} %get-tuple-element.43), channel_id=1, source_target_pairs={{0,2},{1,3},{2,0},{3,1},{4,6},{5,7},{6,4},{7,5},{8,10},{9,11},{10,... | collective-permute-start | bytes 983048 | tf_op jit(solution)/shard_map/reduce_two/ppermute | solution.py:29
  90.4 19.0 %collective-permute-start.20 = (bf16[256,640]{1,0:T(8,128)(2,1)S(1)}, bf16[256,640]{1,0:T(8,128)(2,1)}, u32[]{:S(2)}, u32[]{:S(2)}) collective-permute-start(bf16[256,640]{1,0:T(8,128)(2,1)S(1)} %get-tuple-element.44), channel_id=1, source_target_pairs={{0,1},{1,2},{2,3},{3,0},{4,5},{5,6},{6,7},{7,4},{8,9},{9,10},{10,1... | collective-permute-start | bytes 983048 | tf_op jit(solution)/shard_map/reduce_two/ppermute | solution.py:29
  96.8 13.3 %collective-permute-start.21 = (bf16[256,640]{1,0:T(8,128)(2,1)S(1)}, bf16[256,640]{1,0:T(8,128)(2,1)S(1)}, u32[]{:S(2)}, u32[]{:S(2)}) collective-permute-start(bf16[256,640]{1,0:T(8,128)(2,1)S(1)} %get-tuple-element.45), channel_id=1, source_target_pairs={{0,3},{1,0},{2,1},{3,2},{4,7},{5,4},{6,5},{7,6},{8,11},{9,8},{10,9... | collective-permute-start | bytes 983048 | tf_op jit(solution)/shard_map/reduce_two/ppermute | solution.py:29
  101.7 22.4 %collective-permute-start.11 = (bf16[4,2,128,64]{2,3,0,1:T(8,128)(2,1)}, bf16[4,2,128,64]{2,3,0,1:T(8,128)(2,1)S(1)}, u32[]{:S(2)}, u32[]{:S(2)}) collective-permute-start(bf16[4,2,128,64]{2,3,0,1:T(8,128)(2,1)} %get-tuple-element.79), channel_id=1, source_target_pairs={{0,128},{128,0},{1,129},{129,1},{2,130},{130,2},{3,131},{131,3},{4... | collective-permute-start | bytes 393224 | tf_op jit(solution)/shard_map/out_one/ppermute | solution.py:301
  106.2 6.7 %collective-permute-start.16 = (bf16[64,512]{1,0:T(8,128)(2,1)S(1)}, bf16[64,512]{1,0:T(8,128)(2,1)S(1)}, u32[]{:S(2)}, u32[]{:S(2)}) collective-permute-start(bf16[64,512]{1,0:T(8,128)(2,1)S(1)} %get-tuple-element.71), channel_id=1, source_target_pairs={{0,2},{1,3},{2,0},{3,1},{4,6},{5,7},{6,4},{7,5},{8,10},{9,11},{10,... | collective-permute-start | bytes 196616 | tf_op jit(solution)/shard_map/reduce_two/ppermute | solution.py:29
  108.1 5.8 %collective-permute-start.17 = (bf16[64,512]{1,0:T(8,128)(2,1)S(1)}, bf16[64,512]{1,0:T(8,128)(2,1)S(1)}, u32[]{:S(2)}, u32[]{:S(2)}) collective-permute-start(bf16[64,512]{1,0:T(8,128)(2,1)S(1)} %get-tuple-element.73), channel_id=1, source_target_pairs={{0,1},{1,2},{2,3},{3,0},{4,5},{5,6},{6,7},{7,4},{8,9},{9,10},{10,1... | collective-permute-start | bytes 196616 | tf_op jit(solution)/shard_map/reduce_two/ppermute | solution.py:29
  109.5 6.7 %collective-permute-start.18 = (bf16[64,512]{1,0:T(8,128)(2,1)S(1)}, bf16[64,512]{1,0:T(8,128)(2,1)S(1)}, u32[]{:S(2)}, u32[]{:S(2)}) collective-permute-start(bf16[64,512]{1,0:T(8,128)(2,1)S(1)} %get-tuple-element.72), channel_id=1, source_target_pairs={{0,3},{1,0},{2,1},{3,2},{4,7},{5,4},{6,5},{7,6},{8,11},{9,8},{10,9... | collective-permute-start | bytes 196616 | tf_op jit(solution)/shard_map/reduce_two/ppermute | solution.py:29
  111.8 6.3 %collective-permute-start.22 = (bf16[64,640]{1,0:T(8,128)(2,1)S(1)}, bf16[64,640]{1,0:T(8,128)(2,1)S(1)}, u32[]{:S(2)}, u32[]{:S(2)}) collective-permute-start(bf16[64,640]{1,0:T(8,128)(2,1)S(1)} %get-tuple-element.68), channel_id=1, source_target_pairs={{0,64},{32,96},{64,0},{96,32},{1,65},{33,97},{65,1},{97,33},{2,66}... | collective-permute-start | bytes 245768 | tf_op jit(solution)/shard_map/reduce_two/ppermute | solution.py:29
  112.9 6.0 %collective-permute-start.23 = (bf16[64,640]{1,0:T(8,128)(2,1)S(1)}, bf16[64,640]{1,0:T(8,128)(2,1)S(1)}, u32[]{:S(2)}, u32[]{:S(2)}) collective-permute-start(bf16[64,640]{1,0:T(8,128)(2,1)S(1)} %get-tuple-element.70), channel_id=1, source_target_pairs={{0,32},{32,64},{64,96},{96,0},{1,33},{33,65},{65,97},{97,1},{2,34}... | collective-permute-start | bytes 245768 | tf_op jit(solution)/shard_map/reduce_two/ppermute | solution.py:29
  113.9 5.0 %collective-permute-start.24 = (bf16[64,640]{1,0:T(8,128)(2,1)S(1)}, bf16[64,640]{1,0:T(8,128)(2,1)S(1)}, u32[]{:S(2)}, u32[]{:S(2)}) collective-permute-start(bf16[64,640]{1,0:T(8,128)(2,1)S(1)} %get-tuple-element.69), channel_id=1, source_target_pairs={{0,96},{32,0},{64,32},{96,64},{1,97},{33,1},{65,33},{97,65},{2,98}... | collective-permute-start | bytes 245768 | tf_op jit(solution)/shard_map/reduce_two/ppermute | solution.py:29
  119.6 16.6 %all-to-all-start.1 = ((f32[8,8,1152]{2,1,0:T(8,128)}), f32[8,8,1152]{2,1,0:T(8,128)S(1)}, u32[]{:S(2)}, u32[]{:S(2)}) async-start(f32[8,8,1152]{2,1,0:T(8,128)} %fusion.28), calls=%async_computation.1 | async-start | bytes 589824 | tf_op jit(solution)/shard_map/reduce_two/all_to_all | solution.py:25
  124.3 5.6 %collective-permute-start.25 = (bf16[2,2,128,64]{2,3,1,0:T(8,128)(2,1)S(1)}, bf16[2,2,128,64]{2,3,1,0:T(8,128)(2,1)S(1)}, u32[]{:S(2)}, u32[]{:S(2)}) collective-permute-start(bf16[2,2,128,64]{2,3,1,0:T(8,128)(2,1)S(1)} %get-tuple-element.47), channel_id=1, source_target_pairs={{0,32},{32,64},{64,96},{96,0},{1,33},{33,65},{65,97},{97,1},{2,34}... | collective-permute-start | bytes 196616 | tf_op jit(solution)/shard_map/out_one/ppermute | solution.py:29
  125.6 6.1 %collective-permute-start.26 = (bf16[2,2,128,64]{2,3,1,0:T(8,128)(2,1)S(1)}, bf16[2,2,128,64]{2,3,1,0:T(8,128)(2,1)S(1)}, u32[]{:S(2)}, u32[]{:S(2)}) collective-permute-start(bf16[2,2,128,64]{2,3,1,0:T(8,128)(2,1)S(1)} %get-tuple-element.48), channel_id=1, source_target_pairs={{0,64},{32,96},{64,0},{96,32},{1,65},{33,97},{65,1},{97,33},{2,66}... | collective-permute-start | bytes 196616 | tf_op jit(solution)/shard_map/out_one/ppermute | solution.py:29
  128.8 4.3 %collective-permute-start.27 = (bf16[2,2,128,64]{2,3,1,0:T(8,128)(2,1)S(1)}, bf16[2,2,128,64]{2,3,1,0:T(8,128)(2,1)S(1)}, u32[]{:S(2)}, u32[]{:S(2)}) collective-permute-start(bf16[2,2,128,64]{2,3,1,0:T(8,128)(2,1)S(1)} %get-tuple-element.49), channel_id=1, source_target_pairs={{0,96},{32,0},{64,32},{96,64},{1,97},{33,1},{65,33},{97,65},{2,98}... | collective-permute-start | bytes 196616 | tf_op jit(solution)/shard_map/out_one/ppermute | solution.py:29
  (1 other events, 2.6 us)

commit v2 on v0

--- a/solution.py
+++ b/solution.py
@@ -67,7 +67,7 @@
         return pltpu.make_async_copy(e.at[at, :], e_held.at[j, i], e_sem.at[j, i])
 
     p_copies = [
-        pltpu.make_async_copy(p, p_held.at[j], p_sem.at[j]) for j, p in enumerate((p_mine, p_other))
+        pltpu.make_async_copy(p, p_held.at[j * count : (j + 1) * count, :], p_sem.at[j]) for j, p in enumerate((p_mine, p_other))
     ]
     for i in range(4):
         for j, e in enumerate((e_mine, e_other)):
@@ -95,8 +95,7 @@
 
     def tile(n, carry):
         cols = pl.ds(pl.multiple_of(n * (width // 4), width // 4), width // 4)
-        v = dot(weights[:, :count], p_held[0, :, cols], ((1,), (0,)))
-        v += dot(weights[:, count:], p_held[1, :, cols], ((1,), (0,)))
+        v = dot(weights[...], p_held[:, cols], ((1,), (0,)))
         for i, ref in enumerate(outs):
             ref[:block, cols] = v[i * block : (i + 1) * block, :].astype(ref.dtype)
         return carry
@@ -123,7 +122,7 @@
             pltpu.VMEM((4 * block, 2 * count), bf16),
             pltpu.VMEM((4 * block, 128), f32),
             pltpu.VMEM((2, 4, block, count), bf16),
-            pltpu.VMEM((2, count, width), bf16),
+            pltpu.VMEM((2 * count, width), bf16),
             pltpu.SemaphoreType.DMA((2, 4)),
             pltpu.SemaphoreType.DMA((2,)),
         ],

time: 138 us -> 138 us (level)
  no operation moved by 1% of the time
where the time goes in v2:
time: 138 us
  starting transfers between devices  54.7 us (40%)
  waiting for transfers between devices  38.3 us (28%)
  Pallas kernels  17.9 us (13%)
  other arithmetic  15.2 us (11%)
  matrix products  7.05 us (5%)
  local copies, waits for them, and re-layouts  3.75 us (3%)
    ppermute x26, starting transfers between devices, shift(): return lax.ppermute(v, axis, [(i, (i + k) % n) for i in range(n)])  33.4 us
    ppermute x26, waiting for transfers between devices, shift(): return lax.ppermute(v, axis, [(i, (i + k) % n) for i in range(n)])  22.1 us
    all_to_all x2, starting transfers between devices, swap(): return lax.all_to_all(v, axis, 0, 0, tiled=True)  13.5 us
    pallas_call x2, Pallas kernels, level_one_sums(): pl.pallas_call(sums_kernel, in_specs=[pl.BlockSpec(memory_space=pltpu.SME...  13 us
    all_to_all x2, waiting for transfers between devices, swap(): return lax.all_to_all(v, axis, 0, 0, tiled=True)  8.84 us
    ppermute x1, waiting for transfers between devices, on_device(): lax.ppermute(with_mass(sums[0], block), 'zh', [(0, 1), (1, 0)]).astype(f32)  7.32 us
    dot_general x2, matrix products, dot(): return lax.dot_general(a, b, (dims, ((), ())), preferred_element_type=f32)  7.05 us
    pallas_call x1, Pallas kernels, level_two_sums(): pl.pallas_call(functools.partial(level_two_kernel, count // 256), in_spec...  4.91 us
  transfers between devices with their start and end apart: 30, of which 18 were waited for; matrix products, arithmetic and copies ran while one was open for 13% of the time, Pallas kernels for 5%

profile of v2, /device:TPU:8, one launch (start us, length us, event | category | flops | bytes accessed | tf_op | source)
XLA Modules:
  0.0 137.8 jit_solution(14404866382922629232)
XLA Ops:
  0.7 2.1 %multiply_reduce_fusion = f32[1024]{0:T(1024)S(1)} fusion(bf16[2048,1024]{1,0:T(8,128)(2,1)} %param.7, s32[]{:T(128)S(6)} %select_n.114), kind=kLoop, calls=%fused_computation.4 | loop fusion | flops 3144704 | bytes 2101252 | tf_op jit(solution)/shard_map/scores_one/reduce_sum | solution.py:237
  2.8 4.6 %fusion.4 = (f32[1024]{0:T(1024)S(1)}, f32[1024,1024]{1,0:T(8,128)S(1)}) fusion(f32[1024]{0:T(1024)S(1)} %multiply_reduce_fusion, bf16[1024,1024]{1,0:T(8,128)(2,1)} %p_mine.3, bf16[2048,1024]{1,0:T(8,128)(2,1)} %param.7, s32[]{:T(128)S(6)} %select_n.114), kind=kOutput, calls=%fused_computation.9 | convolution fusion | flops 2151676928 | bytes 8396804 | tf_op jit(solution)/shard_map/scores_one/dot_general | solution.py:37
  7.5 2.4 %fusion = (f32[1024]{0:T(1024)S(1)}, bf16[1024,1024]{1,0:T(8,128)(2,1)}) fusion(f32[1024,1024]{1,0:T(8,128)S(1)} %get-tuple-element.82, f32[1024]{0:T(1024)S(1)} %get-tuple-element.28, f32[1024]{0:T(1024)S(1)} %multiply_reduce_fusion), kind=kLoop, calls=%fused_computation.5 | loop fusion | flops 6290432 | bytes 6303744 | tf_op jit(solution)/shard_map/scores_one/reduce_sum | solution.py:243
  10.0 2.4 %fusion.5 = (f32[1024]{0:T(1024)S(1)}, f32[1024,1024]{1,0:T(8,128)S(1)}) fusion(f32[1024]{0:T(1024)S(1)} %multiply_reduce_fusion, bf16[1024,1024]{1,0:T(8,128)(2,1)S(1)} %collective-permute-done.p_other, bf16[2048,1024]{1,0:T(8,128)(2,1)S(1)} %copy-done.1, s32[]{:T(128)S(6)} %select_n.114), kind=kOutput, calls=%fused_computation.10 | convolution fusion | flops 2151676928 | bytes 8396804 | tf_op jit(solution)/shard_map/scores_one/dot_general | solution.py:37
  12.5 2.4 %fusion.2 = (f32[1024]{0:T(1024)S(1)}, bf16[1024,1024]{1,0:T(8,128)(2,1)}) fusion(f32[1024,1024]{1,0:T(8,128)S(1)} %get-tuple-element.84, f32[1024]{0:T(1024)S(1)} %get-tuple-element.83, f32[1024]{0:T(1024)S(1)} %multiply_reduce_fusion), kind=kLoop, calls=%fused_computation.7 | loop fusion | flops 6290432 | bytes 6303744 | tf_op jit(solution)/shard_map/scores_one/reduce_sum | solution.py:243
  16.9 9.0 %all-to-all-start = ((f32[16,1,1024]{2,1,0:T(1,128)}), f32[16,1,1024]{2,1,0:T(1,128)S(1)}, u32[]{:S(2)}, u32[]{:S(2)}) async-start(f32[16,1,1024]{2,1,0:T(1,128)} %broadcast_in_dim.49), calls=%async_computation | async-start | bytes 131072 | tf_op jit(solution)/shard_map/exchange_softmax/all_to_all | solution.py:25
  25.9 7.0 %all-to-all-done = f32[16,1,1024]{2,1,0:T(1,128)S(1)} async-done(((f32[16,1,1024]{2,1,0:T(1,128)}), f32[16,1,1024]{2,1,0:T(1,128)S(1)}, u32[]{:S(2)}, u32[]{:S(2)}) %all-to-all-start) | async-done | bytes 65568 | tf_op jit(solution)/shard_map/exchange_softmax/all_to_all | solution.py:25
  34.3 6.5 %level_one_sums.3 = (bf16[144,1024]{1,0:T(8,128)(2,1)S(1)}, bf16[144,1024]{1,0:T(8,128)(2,1)S(1)}, bf16[144,1024]{1,0:T(8,128)(2,1)S(1)}, f32[144,1024]{1,0:T(8,128)S(1)}) custom-call(s32[4]{0:T(128)S(1)} %multiply_add_fusion.index, bf16[1024,1024]{1,0:T(8,128)(2,1)} %get-tuple-element.26.e_mine, bf16[1024,1024]{1,0:T(8,128)(2,1)} %get-tuple-element.61.e_other, ...), custom_call_target="tpu_custom_call" | custom-call | flops 2147483648 | bytes 8388608 | tf_op jit(solution)/shard_map/reduce_one/level_one_sums/pallas_call | solution.py:117
  40.8 3.1 %collective-permute-start.6 = (bf16[144,1024]{1,0:T(8,128)(2,1)S(1)}, bf16[144,1024]{1,0:T(8,128)(2,1)S(1)}, u32[]{:S(2)}, u32[]{:S(2)}) collective-permute-start(bf16[144,1024]{1,0:T(8,128)(2,1)S(1)} %get-tuple-element.35), channel_id=1, source_target_pairs={{0,64},{32,96},{64,0},{96,32},{1,65},{33,97},{65,1},{97,33},{2,66}... | collective-permute-start | bytes 884744 | tf_op jit(solution)/shard_map/reduce_one/ppermute | solution.py:29
  44.5 2.6 %collective-permute-start.8 = (bf16[144,1024]{1,0:T(8,128)(2,1)S(1)}, bf16[144,1024]{1,0:T(8,128)(2,1)S(1)}, u32[]{:S(2)}, u32[]{:S(2)}) collective-permute-start(bf16[144,1024]{1,0:T(8,128)(2,1)S(1)} %get-tuple-element.37), channel_id=1, source_target_pairs={{0,96},{32,0},{64,32},{96,64},{1,97},{33,1},{65,33},{97,65},{2,98}... | collective-permute-start | bytes 884744 | tf_op jit(solution)/shard_map/reduce_one/ppermute | solution.py:29
  47.1 6.5 %level_one_sums.2 = (bf16[144,1024]{1,0:T(8,128)(2,1)S(1)}, bf16[144,1024]{1,0:T(8,128)(2,1)S(1)}, bf16[144,1024]{1,0:T(8,128)(2,1)S(1)}, f32[144,1024]{1,0:T(8,128)S(1)}) custom-call(s32[4]{0:T(128)S(1)} %get-tuple-element.56.index, bf16[1024,1024]{1,0:T(8,128)(2,1)} %get-tuple-element.26.e_mine, bf16[1024,1024]{1,0:T(8,128)(2,1)} %get-tuple-element.61.e_other, ...), custom_call_target="tpu_custom_call" | custom-call | flops 2147483648 | bytes 8388608 | tf_op jit(solution)/shard_map/reduce_one/level_one_sums/pallas_call | solution.py:117
  54.6 2.5 %collective-permute-start.5 = (bf16[144,1024]{1,0:T(8,128)(2,1)S(1)}, bf16[144,1024]{1,0:T(8,128)(2,1)S(1)}, u32[]{:S(2)}, u32[]{:S(2)}) collective-permute-start(bf16[144,1024]{1,0:T(8,128)(2,1)S(1)} %get-tuple-element.33), channel_id=1, source_target_pairs={{0,96},{32,0},{64,32},{96,64},{1,97},{33,1},{65,33},{97,65},{2,98}... | collective-permute-start | bytes 884744 | tf_op jit(solution)/shard_map/reduce_one/ppermute | solution.py:29
  57.0 1.5 %collective-permute-done.7 = bf16[144,1024]{1,0:T(8,128)(2,1)S(1)} collective-permute-done((bf16[144,1024]{1,0:T(8,128)(2,1)S(1)}, bf16[144,1024]{1,0:T(8,128)(2,1)S(1)}, u32[]{:S(2)}, u32[]{:S(2)}) %collective-permute-start.7) | collective-permute-done | bytes 294944 | tf_op jit(solution)/shard_map/reduce_one/ppermute | solution.py:29
  59.0 4.6 %collective-permute-start.9 = (bf16[144,1024]{1,0:T(8,128)(2,1)S(1)}, bf16[144,1024]{1,0:T(8,128)(2,1)S(1)}, u32[]{:S(2)}, u32[]{:S(2)}) collective-permute-start(bf16[144,1024]{1,0:T(8,128)(2,1)S(1)} %select_convert_fusion.1), channel_id=1, source_target_pairs={{0,128},{128,0},{1,129},{129,1},{2,130},{130,2},{3,131},{131,3},{4... | collective-permute-start | bytes 884744 | tf_op jit(solution)/shard_map/reduce_one/ppermute | solution.py:261
  63.6 1.6 %collective-permute-done.3 = bf16[144,1024]{1,0:T(8,128)(2,1)S(1)} collective-permute-done((bf16[144,1024]{1,0:T(8,128)(2,1)S(1)}, bf16[144,1024]{1,0:T(8,128)(2,1)S(1)}, u32[]{:S(2)}, u32[]{:S(2)}) %collective-permute-start.3) | collective-permute-done | bytes 294944 | tf_op jit(solution)/shard_map/reduce_one/ppermute | solution.py:29
  65.2 5.2 %collective-permute-done.4 = bf16[144,1024]{1,0:T(8,128)(2,1)S(1)} collective-permute-done((bf16[144,1024]{1,0:T(8,128)(2,1)S(1)}, bf16[144,1024]{1,0:T(8,128)(2,1)S(1)}, u32[]{:S(2)}, u32[]{:S(2)}) %collective-permute-start.4) | collective-permute-done | bytes 294944 | tf_op jit(solution)/shard_map/reduce_one/ppermute | solution.py:29
  70.6 7.3 %collective-permute-done.9 = bf16[144,1024]{1,0:T(8,128)(2,1)S(1)} collective-permute-done((bf16[144,1024]{1,0:T(8,128)(2,1)S(1)}, bf16[144,1024]{1,0:T(8,128)(2,1)S(1)}, u32[]{:S(2)}, u32[]{:S(2)}) %collective-permute-start.9) | collective-permute-done | bytes 294944 | tf_op jit(solution)/shard_map/reduce_one/ppermute | solution.py:261
  81.0 4.9 %level_two_sums.1 = (bf16[256,512]{1,0:T(8,128)(2,1)S(1)}, bf16[256,512]{1,0:T(8,128)(2,1)S(1)}, bf16[256,512]{1,0:T(8,128)(2,1)S(1)}, f32[256,512]{1,0:T(8,128)...) custom-call(s32[9]{0:T(128)S(1)} %pad_add_fusion.place, ...), custom_call_target="tpu_custom_call" | custom-call | flops 2147483648 | bytes 8388608 | tf_op jit(solution)/shard_map/scores_two/level_two_sums/pallas_call | solution.py:200
  87.0 2.7 %collective-permute-start.14 = (bf16[256,512]{1,0:T(8,128)(2,1)S(1)}, bf16[256,512]{1,0:T(8,128)(2,1)}, u32[]{:S(2)}, u32[]{:S(2)}) collective-permute-start(bf16[256,512]{1,0:T(8,128)(2,1)S(1)} %get-tuple-element.40), channel_id=1, source_target_pairs={{0,32},{32,64},{64,96},{96,0},{1,33},{33,65},{65,97},{97,1},{2,34}... | collective-permute-start | bytes 786440 | tf_op jit(solution)/shard_map/reduce_two/ppermute | solution.py:29
  90.4 2.9 %collective-permute-start.20 = (bf16[256,640]{1,0:T(8,128)(2,1)S(1)}, bf16[256,640]{1,0:T(8,128)(2,1)}, u32[]{:S(2)}, u32[]{:S(2)}) collective-permute-start(bf16[256,640]{1,0:T(8,128)(2,1)S(1)} %get-tuple-element.44), channel_id=1, source_target_pairs={{0,1},{1,2},{2,3},{3,0},{4,5},{5,6},{6,7},{7,4},{8,9},{9,10},{10,1... | collective-permute-start | bytes 983048 | tf_op jit(solution)/shard_map/reduce_two/ppermute | solution.py:29
  95.1 1.6 %collective-permute-done.13 = bf16[256,512]{1,0:T(8,128)(2,1)} collective-permute-done((bf16[256,512]{1,0:T(8,128)(2,1)S(1)}, bf16[256,512]{1,0:T(8,128)(2,1)}, u32[]{:S(2)}, u32[]{:S(2)}) %collective-permute-start.13) | collective-permute-done | bytes 262176 | tf_op jit(solution)/shard_map/reduce_two/ppermute | solution.py:29
  96.8 1.5 %collective-permute-start.21 = (bf16[256,640]{1,0:T(8,128)(2,1)S(1)}, bf16[256,640]{1,0:T(8,128)(2,1)S(1)}, u32[]{:S(2)}, u32[]{:S(2)}) collective-permute-start(bf16[256,640]{1,0:T(8,128)(2,1)S(1)} %get-tuple-element.45), channel_id=1, source_target_pairs={{0,3},{1,0},{2,1},{3,2},{4,7},{5,4},{6,5},{7,6},{8,11},{9,8},{10,9... | collective-permute-start | bytes 983048 | tf_op jit(solution)/shard_map/reduce_two/ppermute | solution.py:29
  98.3 3.5 %collective-permute-done.14 = bf16[256,512]{1,0:T(8,128)(2,1)} collective-permute-done((bf16[256,512]{1,0:T(8,128)(2,1)S(1)}, bf16[256,512]{1,0:T(8,128)(2,1)}, u32[]{:S(2)}, u32[]{:S(2)}) %collective-permute-start.14) | collective-permute-done | bytes 262176 | tf_op jit(solution)/shard_map/reduce_two/ppermute | solution.py:29
  101.7 3.2 %collective-permute-start.11 = (bf16[4,2,128,64]{2,3,0,1:T(8,128)(2,1)}, bf16[4,2,128,64]{2,3,0,1:T(8,128)(2,1)S(1)}, u32[]{:S(2)}, u32[]{:S(2)}) collective-permute-start(bf16[4,2,128,64]{2,3,0,1:T(8,128)(2,1)} %get-tuple-element.79), channel_id=1, source_target_pairs={{0,128},{128,0},{1,129},{129,1},{2,130},{130,2},{3,131},{131,3},{4... | collective-permute-start | bytes 393224 | tf_op jit(solution)/shard_map/out_one/ppermute | solution.py:298
  106.2 1.9 %collective-permute-start.16 = (bf16[64,512]{1,0:T(8,128)(2,1)S(1)}, bf16[64,512]{1,0:T(8,128)(2,1)S(1)}, u32[]{:S(2)}, u32[]{:S(2)}) collective-permute-start(bf16[64,512]{1,0:T(8,128)(2,1)S(1)} %get-tuple-element.71), channel_id=1, source_target_pairs={{0,2},{1,3},{2,0},{3,1},{4,6},{5,7},{6,4},{7,5},{8,10},{9,11},{10,... | collective-permute-start | bytes 196616 | tf_op jit(solution)/shard_map/reduce_two/ppermute | solution.py:29
  113.8 2.3 %collective-permute-start.24 = (bf16[64,640]{1,0:T(8,128)(2,1)S(1)}, bf16[64,640]{1,0:T(8,128)(2,1)S(1)}, u32[]{:S(2)}, u32[]{:S(2)}) collective-permute-start(bf16[64,640]{1,0:T(8,128)(2,1)S(1)} %get-tuple-element.69), channel_id=1, source_target_pairs={{0,96},{32,0},{64,32},{96,64},{1,97},{33,1},{65,33},{97,65},{2,98}... | collective-permute-start | bytes 245768 | tf_op jit(solution)/shard_map/reduce_two/ppermute | solution.py:29
  116.1 1.9 %collective-permute-done.22 = bf16[64,640]{1,0:T(8,128)(2,1)S(1)} collective-permute-done((bf16[64,640]{1,0:T(8,128)(2,1)S(1)}, bf16[64,640]{1,0:T(8,128)(2,1)S(1)}, u32[]{:S(2)}, u32[]{:S(2)}) %collective-permute-start.22) | collective-permute-done | bytes 81952 | tf_op jit(solution)/shard_map/reduce_two/ppermute | solution.py:29
  119.6 4.5 %all-to-all-start.1 = ((f32[8,8,1152]{2,1,0:T(8,128)}), f32[8,8,1152]{2,1,0:T(8,128)S(1)}, u32[]{:S(2)}, u32[]{:S(2)}) async-start(f32[8,8,1152]{2,1,0:T(8,128)} %fusion.28), calls=%async_computation.1 | async-start | bytes 589824 | tf_op jit(solution)/shard_map/reduce_two/all_to_all | solution.py:25
  125.6 3.2 %collective-permute-start.26 = (bf16[2,2,128,64]{2,3,1,0:T(8,128)(2,1)S(1)}, bf16[2,2,128,64]{2,3,1,0:T(8,128)(2,1)S(1)}, u32[]{:S(2)}, u32[]{:S(2)}) collective-permute-start(bf16[2,2,128,64]{2,3,1,0:T(8,128)(2,1)S(1)} %get-tuple-element.48), channel_id=1, source_target_pairs={{0,64},{32,96},{64,0},{96,32},{1,65},{33,97},{65,1},{97,33},{2,66}... | collective-permute-start | bytes 196616 | tf_op jit(solution)/shard_map/out_one/ppermute | solution.py:29
  129.8 1.9 %collective-permute-done.26 = bf16[2,2,128,64]{2,3,1,0:T(8,128)(2,1)S(1)} collective-permute-done((bf16[2,2,128,64]{2,3,1,0:T(8,128)(2,1)S(1)}, bf16[2,2,128,64]{2,3,1,0:T(8,128)(2,1)S(1)}, u32[]{:S(2)}, u32[]{:S(2)}) %collective-permute-start.26) | collective-permute-done | bytes 65568 | tf_op jit(solution)/shard_map/out_one/ppermute | solution.py:29
  134.4 1.8 %all-to-all-done.1 = f32[8,8,1152]{2,1,0:T(8,128)S(1)} async-done(((f32[8,8,1152]{2,1,0:T(8,128)}), f32[8,8,1152]{2,1,0:T(8,128)S(1)}, u32[]{:S(2)}, u32[]{:S(2)}) %all-to-all-start.1) | async-done | bytes 294944 | tf_op jit(solution)/shard_map/reduce_two/all_to_all | solution.py:25
  136.4 1.4 %fusion.18 = bf16[8,1024]{1,0:T(8,128)(2,1)} fusion(f32[8,1152]{1,0:T(8,128)S(1)} %reduce_sum.59, f32[8]{0:T(128)S(1)} %fusion.22, bf16[2048,1024]{1,0:T(8,128)(2,1)} %table_far.1, s32[]{:T(128)S(6)} %select_n.137), kind=kLoop, calls=%fused_computation.51 | loop fusion | flops 40960 | bytes 65572 | tf_op jit(solution)/shard_map/finish_two/convert_element_type | solution.py:309
  (90 shorter events, 26.3 us)
Async XLA Ops:
  0.6 9.3 %collective-permute-start = (bf16[1024,1024]{1,0:T(8,128)(2,1)}, bf16[1024,1024]{1,0:T(8,128)(2,1)S(1)}, u32[]{:S(2)}, u32[]{:S(2)}) collective-permute-start(bf16[1024,1024]{1,0:T(8,128)(2,1)} %p_mine.3), channel_id=1, source_target_pairs={{0,16},{16,0},{1,17},{17,1},{2,18},{18,2},{3,19},{19,3},{4,20},{20... | collective-permute-start | bytes 6291464 | tf_op jit(solution)/shard_map/scores_one/ppermute | solution.py:29
  7.4 2.6 %copy-start.1 = (bf16[2048,1024]{1,0:T(8,128)(2,1)S(1)}, bf16[2048,1024]{1,0:T(8,128)(2,1)}, u32[]{:S(2)}) copy-start(bf16[2048,1024]{1,0:T(8,128)(2,1)} %param.7) | copy-start | bytes 12582916
  12.5 13.4 %copy-start.2 = (s32[4]{0:T(128)S(1)}, s32[4]{0:T(128)}, u32[]{:S(2)}) copy-start(s32[4]{0:T(128)} %constant.146.clone) | copy-start | bytes 52
  14.9 1.3 collective-permute-start.1
  16.9 16.0 %all-to-all-start = ((f32[16,1,1024]{2,1,0:T(1,128)}), f32[16,1,1024]{2,1,0:T(1,128)S(1)}, u32[]{:S(2)}, u32[]{:S(2)}) async-start(f32[16,1,1024]{2,1,0:T(1,128)} %broadcast_in_dim.49), calls=%async_computation | async-start | bytes 131072 | tf_op jit(solution)/shard_map/exchange_softmax/all_to_all | solution.py:25
  33.0 1.3 collective-permute-start.2
  40.8 13.8 %collective-permute-start.6 = (bf16[144,1024]{1,0:T(8,128)(2,1)S(1)}, bf16[144,1024]{1,0:T(8,128)(2,1)S(1)}, u32[]{:S(2)}, u32[]{:S(2)}) collective-permute-start(bf16[144,1024]{1,0:T(8,128)(2,1)S(1)} %get-tuple-element.35), channel_id=1, source_target_pairs={{0,64},{32,96},{64,0},{96,32},{1,65},{33,97},{65,1},{97,33},{2,66}... | collective-permute-start | bytes 884744 | tf_op jit(solution)/shard_map/reduce_one/ppermute | solution.py:29
  43.9 14.6 %collective-permute-start.7 = (bf16[144,1024]{1,0:T(8,128)(2,1)S(1)}, bf16[144,1024]{1,0:T(8,128)(2,1)S(1)}, u32[]{:S(2)}, u32[]{:S(2)}) collective-permute-start(bf16[144,1024]{1,0:T(8,128)(2,1)S(1)} %get-tuple-element.36), channel_id=1, source_target_pairs={{0,32},{32,64},{64,96},{96,0},{1,33},{33,65},{65,97},{97,1},{2,34}... | collective-permute-start | bytes 884744 | tf_op jit(solution)/shard_map/reduce_one/ppermute | solution.py:29
  44.5 14.2 %collective-permute-start.8 = (bf16[144,1024]{1,0:T(8,128)(2,1)S(1)}, bf16[144,1024]{1,0:T(8,128)(2,1)S(1)}, u32[]{:S(2)}, u32[]{:S(2)}) collective-permute-start(bf16[144,1024]{1,0:T(8,128)(2,1)S(1)} %get-tuple-element.37), channel_id=1, source_target_pairs={{0,96},{32,0},{64,32},{96,64},{1,97},{33,1},{65,33},{97,65},{2,98}... | collective-permute-start | bytes 884744 | tf_op jit(solution)/shard_map/reduce_one/ppermute | solution.py:29
  53.6 11.6 %collective-permute-start.3 = (bf16[144,1024]{1,0:T(8,128)(2,1)S(1)}, bf16[144,1024]{1,0:T(8,128)(2,1)S(1)}, u32[]{:S(2)}, u32[]{:S(2)}) collective-permute-start(bf16[144,1024]{1,0:T(8,128)(2,1)S(1)} %get-tuple-element.31), channel_id=1, source_target_pairs={{0,64},{32,96},{64,0},{96,32},{1,65},{33,97},{65,1},{97,33},{2,66}... | collective-permute-start | bytes 884744 | tf_op jit(solution)/shard_map/reduce_one/ppermute | solution.py:29
  53.7 16.7 %collective-permute-start.4 = (bf16[144,1024]{1,0:T(8,128)(2,1)S(1)}, bf16[144,1024]{1,0:T(8,128)(2,1)S(1)}, u32[]{:S(2)}, u32[]{:S(2)}) collective-permute-start(bf16[144,1024]{1,0:T(8,128)(2,1)S(1)} %get-tuple-element.32), channel_id=1, source_target_pairs={{0,32},{32,64},{64,96},{96,0},{1,33},{33,65},{65,97},{97,1},{2,34}... | collective-permute-start | bytes 884744 | tf_op jit(solution)/shard_map/reduce_one/ppermute | solution.py:29
  54.6 16.0 %collective-permute-start.5 = (bf16[144,1024]{1,0:T(8,128)(2,1)S(1)}, bf16[144,1024]{1,0:T(8,128)(2,1)S(1)}, u32[]{:S(2)}, u32[]{:S(2)}) collective-permute-start(bf16[144,1024]{1,0:T(8,128)(2,1)S(1)} %get-tuple-element.33), channel_id=1, source_target_pairs={{0,96},{32,0},{64,32},{96,64},{1,97},{33,1},{65,33},{97,65},{2,98}... | collective-permute-start | bytes 884744 | tf_op jit(solution)/shard_map/reduce_one/ppermute | solution.py:29
  59.0 18.9 %collective-permute-start.9 = (bf16[144,1024]{1,0:T(8,128)(2,1)S(1)}, bf16[144,1024]{1,0:T(8,128)(2,1)S(1)}, u32[]{:S(2)}, u32[]{:S(2)}) collective-permute-start(bf16[144,1024]{1,0:T(8,128)(2,1)S(1)} %select_convert_fusion.1), channel_id=1, source_target_pairs={{0,128},{128,0},{1,129},{129,1},{2,130},{130,2},{3,131},{131,3},{4... | collective-permute-start | bytes 884744 | tf_op jit(solution)/shard_map/reduce_one/ppermute | solution.py:261
  79.2 1.8 %collective-permute-start.10 = (bf16[128,1024]{1,0:T(8,128)(2,1)S(1)}, bf16[128,1024]{1,0:T(8,128)(2,1)S(1)}, u32[]{:S(2)}, u32[]{:S(2)}) collective-permute-start(bf16[128,1024]{1,0:T(8,128)(2,1)S(1)} %fusion.11.rows_mine), channel_id=1, source_target_pairs={{0,16},{16,0},{1,17},{17,1},{2,18},{18,2},{3,19},{19,3},{4,20},{20... | collective-permute-start | bytes 786440 | tf_op jit(solution)/shard_map/finish_one/ppermute | solution.py:29
  79.6 1.4 %collective-permute-start.12 = (f32[128]{0:T(128)S(1)}, f32[128]{0:T(128)S(1)}, u32[]{:S(2)}, u32[]{:S(2)}) collective-permute-start(f32[128]{0:T(128)S(1)} %bitcast.68), channel_id=1, source_target_pairs={{0,16},{16,0},{1,17},{17,1},{2,18},{18,2},{3,19},{19,3},{4,20},{20... | collective-permute-start | bytes 1544 | tf_op jit(solution)/shard_map/finish_one/ppermute | solution.py:29
  85.9 10.9 %collective-permute-start.13 = (bf16[256,512]{1,0:T(8,128)(2,1)S(1)}, bf16[256,512]{1,0:T(8,128)(2,1)}, u32[]{:S(2)}, u32[]{:S(2)}) collective-permute-start(bf16[256,512]{1,0:T(8,128)(2,1)S(1)} %get-tuple-element.39), channel_id=1, source_target_pairs={{0,64},{32,96},{64,0},{96,32},{1,65},{33,97},{65,1},{97,33},{2,66}... | collective-permute-start | bytes 786440 | tf_op jit(solution)/shard_map/reduce_two/ppermute | solution.py:29
  87.0 14.7 %collective-permute-start.14 = (bf16[256,512]{1,0:T(8,128)(2,1)S(1)}, bf16[256,512]{1,0:T(8,128)(2,1)}, u32[]{:S(2)}, u32[]{:S(2)}) collective-permute-start(bf16[256,512]{1,0:T(8,128)(2,1)S(1)} %get-tuple-element.40), channel_id=1, source_target_pairs={{0,32},{32,64},{64,96},{96,0},{1,33},{33,65},{65,97},{97,1},{2,34}... | collective-permute-start | bytes 786440 | tf_op jit(solution)/shard_map/reduce_two/ppermute | solution.py:29
  89.7 15.2 %collective-permute-start.15 = (bf16[256,512]{1,0:T(8,128)(2,1)S(1)}, bf16[256,512]{1,0:T(8,128)(2,1)}, u32[]{:S(2)}, u32[]{:S(2)}) collective-permute-start(bf16[256,512]{1,0:T(8,128)(2,1)S(1)} %get-tuple-element.41), channel_id=1, source_target_pairs={{0,96},{32,0},{64,32},{96,64},{1,97},{33,1},{65,33},{97,65},{2,98}... | collective-permute-start | bytes 786440 | tf_op jit(solution)/shard_map/reduce_two/ppermute | solution.py:29
  90.3 17.8 %collective-permute-start.19 = (bf16[256,640]{1,0:T(8,128)(2,1)S(1)}, bf16[256,640]{1,0:T(8,128)(2,1)}, u32[]{:S(2)}, u32[]{:S(2)}) collective-permute-start(bf16[256,640]{1,0:T(8,128)(2,1)S(1)} %get-tuple-element.43), channel_id=1, source_target_pairs={{0,2},{1,3},{2,0},{3,1},{4,6},{5,7},{6,4},{7,5},{8,10},{9,11},{10,... | collective-permute-start | bytes 983048 | tf_op jit(solution)/shard_map/reduce_two/ppermute | solution.py:29
  90.4 19.1 %collective-permute-start.20 = (bf16[256,640]{1,0:T(8,128)(2,1)S(1)}, bf16[256,640]{1,0:T(8,128)(2,1)}, u32[]{:S(2)}, u32[]{:S(2)}) collective-permute-start(bf16[256,640]{1,0:T(8,128)(2,1)S(1)} %get-tuple-element.44), channel_id=1, source_target_pairs={{0,1},{1,2},{2,3},{3,0},{4,5},{5,6},{6,7},{7,4},{8,9},{9,10},{10,1... | collective-permute-start | bytes 983048 | tf_op jit(solution)/shard_map/reduce_two/ppermute | solution.py:29
  96.8 13.3 %collective-permute-start.21 = (bf16[256,640]{1,0:T(8,128)(2,1)S(1)}, bf16[256,640]{1,0:T(8,128)(2,1)S(1)}, u32[]{:S(2)}, u32[]{:S(2)}) collective-permute-start(bf16[256,640]{1,0:T(8,128)(2,1)S(1)} %get-tuple-element.45), channel_id=1, source_target_pairs={{0,3},{1,0},{2,1},{3,2},{4,7},{5,4},{6,5},{7,6},{8,11},{9,8},{10,9... | collective-permute-start | bytes 983048 | tf_op jit(solution)/shard_map/reduce_two/ppermute | solution.py:29
  101.7 22.4 %collective-permute-start.11 = (bf16[4,2,128,64]{2,3,0,1:T(8,128)(2,1)}, bf16[4,2,128,64]{2,3,0,1:T(8,128)(2,1)S(1)}, u32[]{:S(2)}, u32[]{:S(2)}) collective-permute-start(bf16[4,2,128,64]{2,3,0,1:T(8,128)(2,1)} %get-tuple-element.79), channel_id=1, source_target_pairs={{0,128},{128,0},{1,129},{129,1},{2,130},{130,2},{3,131},{131,3},{4... | collective-permute-start | bytes 393224 | tf_op jit(solution)/shard_map/out_one/ppermute | solution.py:298
  106.2 6.7 %collective-permute-start.16 = (bf16[64,512]{1,0:T(8,128)(2,1)S(1)}, bf16[64,512]{1,0:T(8,128)(2,1)S(1)}, u32[]{:S(2)}, u32[]{:S(2)}) collective-permute-start(bf16[64,512]{1,0:T(8,128)(2,1)S(1)} %get-tuple-element.71), channel_id=1, source_target_pairs={{0,2},{1,3},{2,0},{3,1},{4,6},{5,7},{6,4},{7,5},{8,10},{9,11},{10,... | collective-permute-start | bytes 196616 | tf_op jit(solution)/shard_map/reduce_two/ppermute | solution.py:29
  108.1 5.7 %collective-permute-start.17 = (bf16[64,512]{1,0:T(8,128)(2,1)S(1)}, bf16[64,512]{1,0:T(8,128)(2,1)S(1)}, u32[]{:S(2)}, u32[]{:S(2)}) collective-permute-start(bf16[64,512]{1,0:T(8,128)(2,1)S(1)} %get-tuple-element.73), channel_id=1, source_target_pairs={{0,1},{1,2},{2,3},{3,0},{4,5},{5,6},{6,7},{7,4},{8,9},{9,10},{10,1... | collective-permute-start | bytes 196616 | tf_op jit(solution)/shard_map/reduce_two/ppermute | solution.py:29
  109.5 6.6 %collective-permute-start.18 = (bf16[64,512]{1,0:T(8,128)(2,1)S(1)}, bf16[64,512]{1,0:T(8,128)(2,1)S(1)}, u32[]{:S(2)}, u32[]{:S(2)}) collective-permute-start(bf16[64,512]{1,0:T(8,128)(2,1)S(1)} %get-tuple-element.72), channel_id=1, source_target_pairs={{0,3},{1,0},{2,1},{3,2},{4,7},{5,4},{6,5},{7,6},{8,11},{9,8},{10,9... | collective-permute-start | bytes 196616 | tf_op jit(solution)/shard_map/reduce_two/ppermute | solution.py:29
  111.7 6.2 %collective-permute-start.22 = (bf16[64,640]{1,0:T(8,128)(2,1)S(1)}, bf16[64,640]{1,0:T(8,128)(2,1)S(1)}, u32[]{:S(2)}, u32[]{:S(2)}) collective-permute-start(bf16[64,640]{1,0:T(8,128)(2,1)S(1)} %get-tuple-element.68), channel_id=1, source_target_pairs={{0,64},{32,96},{64,0},{96,32},{1,65},{33,97},{65,1},{97,33},{2,66}... | collective-permute-start | bytes 245768 | tf_op jit(solution)/shard_map/reduce_two/ppermute | solution.py:29
  112.8 6.0 %collective-permute-start.23 = (bf16[64,640]{1,0:T(8,128)(2,1)S(1)}, bf16[64,640]{1,0:T(8,128)(2,1)S(1)}, u32[]{:S(2)}, u32[]{:S(2)}) collective-permute-start(bf16[64,640]{1,0:T(8,128)(2,1)S(1)} %get-tuple-element.70), channel_id=1, source_target_pairs={{0,32},{32,64},{64,96},{96,0},{1,33},{33,65},{65,97},{97,1},{2,34}... | collective-permute-start | bytes 245768 | tf_op jit(solution)/shard_map/reduce_two/ppermute | solution.py:29
  113.8 5.0 %collective-permute-start.24 = (bf16[64,640]{1,0:T(8,128)(2,1)S(1)}, bf16[64,640]{1,0:T(8,128)(2,1)S(1)}, u32[]{:S(2)}, u32[]{:S(2)}) collective-permute-start(bf16[64,640]{1,0:T(8,128)(2,1)S(1)} %get-tuple-element.69), channel_id=1, source_target_pairs={{0,96},{32,0},{64,32},{96,64},{1,97},{33,1},{65,33},{97,65},{2,98}... | collective-permute-start | bytes 245768 | tf_op jit(solution)/shard_map/reduce_two/ppermute | solution.py:29
  119.6 16.6 %all-to-all-start.1 = ((f32[8,8,1152]{2,1,0:T(8,128)}), f32[8,8,1152]{2,1,0:T(8,128)S(1)}, u32[]{:S(2)}, u32[]{:S(2)}) async-start(f32[8,8,1152]{2,1,0:T(8,128)} %fusion.28), calls=%async_computation.1 | async-start | bytes 589824 | tf_op jit(solution)/shard_map/reduce_two/all_to_all | solution.py:25
  124.2 5.6 %collective-permute-start.25 = (bf16[2,2,128,64]{2,3,1,0:T(8,128)(2,1)S(1)}, bf16[2,2,128,64]{2,3,1,0:T(8,128)(2,1)S(1)}, u32[]{:S(2)}, u32[]{:S(2)}) collective-permute-start(bf16[2,2,128,64]{2,3,1,0:T(8,128)(2,1)S(1)} %get-tuple-element.47), channel_id=1, source_target_pairs={{0,32},{32,64},{64,96},{96,0},{1,33},{33,65},{65,97},{97,1},{2,34}... | collective-permute-start | bytes 196616 | tf_op jit(solution)/shard_map/out_one/ppermute | solution.py:29
  125.6 6.1 %collective-permute-start.26 = (bf16[2,2,128,64]{2,3,1,0:T(8,128)(2,1)S(1)}, bf16[2,2,128,64]{2,3,1,0:T(8,128)(2,1)S(1)}, u32[]{:S(2)}, u32[]{:S(2)}) collective-permute-start(bf16[2,2,128,64]{2,3,1,0:T(8,128)(2,1)S(1)} %get-tuple-element.48), channel_id=1, source_target_pairs={{0,64},{32,96},{64,0},{96,32},{1,65},{33,97},{65,1},{97,33},{2,66}... | collective-permute-start | bytes 196616 | tf_op jit(solution)/shard_map/out_one/ppermute | solution.py:29
  128.8 4.3 %collective-permute-start.27 = (bf16[2,2,128,64]{2,3,1,0:T(8,128)(2,1)S(1)}, bf16[2,2,128,64]{2,3,1,0:T(8,128)(2,1)S(1)}, u32[]{:S(2)}, u32[]{:S(2)}) collective-permute-start(bf16[2,2,128,64]{2,3,1,0:T(8,128)(2,1)S(1)} %get-tuple-element.49), channel_id=1, source_target_pairs={{0,96},{32,0},{64,32},{96,64},{1,97},{33,1},{65,33},{97,65},{2,98}... | collective-permute-start | bytes 196616 | tf_op jit(solution)/shard_map/out_one/ppermute | solution.py:29
  (1 other events, 2.6 us)
